TPU v7x, 512 devices: a whole 4x8x8 slice. The times are simulated.
512 devices in a mesh: dp: 32 (over z, x), ctx: 16 (over y, core).
Axes of the slice: x: 4, y: 8, z: 8, core: 2. Of those that a mesh axis runs over, the one named last changes fastest.
Arguments:
- hidden: bfloat16 [32, 2048, 4096], P('dp', 'ctx'), may hold values from -6 to 6
- queries: bfloat16 [32, 2048, 2048], P('dp', 'ctx'), may hold values from -9 to 9
- keys: bfloat16 [32, 2048, 512], P('dp', 'ctx'), may hold values from -9 to 9
- cotangent: bfloat16 [32, 2048, 2048], P('dp', 'ctx'), may hold values from -4 to 4
- value_weight: bfloat16 [4096, 512], P('ctx'), may hold values from -0.09375 to 0.09375
- doc_ids: int32 [32, 2048], P('dp'), may hold values from 0 to 15, never falling along the last dimension, each value on 1 to 1024 neighbouring positions
- span_order: int32 [32, 32], P('dp'), may hold values from 0 to 31, each once within a row
Outputs:
- attention_out: bfloat16 [32, 2048, 2048], P('dp', 'ctx')
- query_grads: bfloat16 [32, 2048, 2048], P('dp', 'ctx')
- key_grads: bfloat16 [32, 2048, 512], P('dp', 'ctx')
- input_grads: bfloat16 [32, 2048, 4096], P('dp', 'ctx')
- weight_grads: bfloat16 [4096, 512], P('ctx')
Inputs may be any that keep to these rules, and one draw needn't show every extreme that they name: `span_order`: each row lists every span of its sequence once; entries r * 2 to r * 2 + 1 are the spans of 64 positions held by ctx rank r, in order. `doc_ids`: each row never falls along the sequence; every document has at least one position and at most half of 2048, one exactly that many.
All inputs are finite; a program needn't handle non-finite values.
Results may differ from a plain program's by a relative error of at most 0.025.
The roundings to bfloat16 on the way count: a program that leaves them out, or rounds other values in their place, can miss the bound.
Values may be sent and summed in bfloat16 or wider, within the bound.
A program may use at most 64 MiB of HBM per device.

v0:
```python
import math

import jax
import jax.numpy as jnp
from jax import lax
from jax.experimental import pallas as pl
from jax.experimental.pallas import tpu as pltpu
from jax.sharding import PartitionSpec as P

HQ = 16
KVH = 4
HD = 128
CPR = 2
SPAN = 64
CHUNK = 256
GROUP = HQ // KVH
ROWS = SPAN * GROUP
INV_ROOT = 1.0 / math.sqrt(HD)
LOG2_SCALE = INV_ROOT * math.log2(math.e)
FAR = -1e30

NT = (((1,), (1,)), ((), ()))
TN = (((0,), (0,)), ((), ()))
NN = (((1,), (0,)), ((), ()))


def mm(a, b, dims):
    return lax.dot_general(a, b, dims, preferred_element_type=jnp.float32)


def attention_kernel(
    spans_ref,
    bounds_ref,
    q_ref,
    do_ref,
    kv_ref,
    start_ref,
    pos_ref,
    o_ref,
    dq_ref,
    dkv_ref,
    seq_ref,
    acc_ref,
    s_ref,
    p_ref,
    t_ref,
):
    num_spans = spans_ref.shape[0]
    kv_width = KVH * HD

    def to_sequence(i, _):
        src = pl.multiple_of(i * SPAN, SPAN)
        dst = pl.multiple_of(spans_ref[i] * SPAN, SPAN)
        seq_ref[pl.ds(dst, SPAN), :] = kv_ref[pl.ds(src, SPAN), :]
        acc_ref[pl.ds(src, SPAN), :] = jnp.zeros((SPAN, 2 * kv_width), jnp.float32)
        return 0

    lax.fori_loop(0, num_spans, to_sequence, 0)

    def rows_of(ref, span, head):
        return jnp.concatenate(
            [
                ref[
                    span * SPAN : (span + 1) * SPAN,
                    (head * GROUP + j) * HD : (head * GROUP + j + 1) * HD,
                ]
                for j in range(GROUP)
            ],
            axis=0,
        )

    def write_rows(ref, span, head, block):
        for j in range(GROUP):
            ref[
                span * SPAN : (span + 1) * SPAN,
                (head * GROUP + j) * HD : (head * GROUP + j + 1) * HD,
            ] = block[j * SPAN : (j + 1) * SPAN, :]

    def key_cols(head):
        return slice(head * HD, (head + 1) * HD)

    def value_cols(head):
        return slice(kv_width + head * HD, kv_width + (head + 1) * HD)

    for span in range(CPR):
        first = bounds_ref[2 * span]
        last = bounds_ref[2 * span + 1]
        start = start_ref[span : span + 1, :]
        pos = pos_ref[span : span + 1, :]

        def score_step(c, carry):
            rows = pl.ds(pl.multiple_of(c * CHUNK, CHUNK), CHUNK)
            key_pos = lax.broadcasted_iota(jnp.int32, (CHUNK, ROWS), 0) + c * CHUNK
            keep = (key_pos >= start) & (key_pos <= pos)
            out = []
            for head in range(KVH):
                top, total = carry[head]
                s = mm(seq_ref[rows, key_cols(head)], rows_of(q_ref, span, head), NT)
                s = jnp.where(keep, s * LOG2_SCALE, FAR)
                s_ref[head, c] = s
                new_top = jnp.maximum(top, jnp.max(s, axis=0, keepdims=True))
                new_total = total * jnp.exp2(top - new_top) + jnp.sum(
                    jnp.exp2(s - new_top), axis=0, keepdims=True
                )
                out.append((new_top, new_total))
            return tuple(out)

        empty = (jnp.full((1, ROWS), FAR, jnp.float32), jnp.zeros((1, ROWS), jnp.float32))
        stats = lax.fori_loop(first, last, score_step, (empty,) * KVH)
        log_total = [top + jnp.log2(total) for top, total in stats]
        t_ref[...] = jnp.zeros_like(t_ref)

        def value_step(c, _):
            rows = pl.ds(pl.multiple_of(c * CHUNK, CHUNK), CHUNK)
            for head in range(KVH):
                p = jnp.exp2(s_ref[head, c] - log_total[head]).astype(jnp.bfloat16)
                p_ref[head, c] = p
                t_ref[head] += mm(seq_ref[rows, value_cols(head)], p, TN)
                acc_ref[rows, value_cols(head)] += mm(p, rows_of(do_ref, span, head), NN)
            return 0

        lax.fori_loop(first, last, value_step, 0)
        delta = []
        for head in range(KVH):
            out_t = t_ref[head].astype(jnp.bfloat16).astype(jnp.float32)
            grad_t = rows_of(do_ref, span, head).astype(jnp.float32).T
            delta.append(jnp.sum(out_t * grad_t, axis=0, keepdims=True))
            write_rows(o_ref, span, head, out_t.T.astype(jnp.bfloat16))
        t_ref[...] = jnp.zeros_like(t_ref)

        def grad_step(c, _):
            rows = pl.ds(pl.multiple_of(c * CHUNK, CHUNK), CHUNK)
            for head in range(KVH):
                dp = mm(seq_ref[rows, value_cols(head)], rows_of(do_ref, span, head), NT)
                ds = (p_ref[head, c].astype(jnp.float32) * (dp - delta[head])).astype(jnp.bfloat16)
                t_ref[head] += mm(seq_ref[rows, key_cols(head)], ds, TN)
                acc_ref[rows, key_cols(head)] += mm(ds, rows_of(q_ref, span, head), NN)
            return 0

        lax.fori_loop(first, last, grad_step, 0)
        for head in range(KVH):
            write_rows(dq_ref, span, head, (t_ref[head] * INV_ROOT).T.astype(jnp.bfloat16))

    def to_layout(i, _):
        dst = pl.multiple_of(i * SPAN, SPAN)
        src = pl.multiple_of(spans_ref[i] * SPAN, SPAN)
        dkv_ref[pl.ds(dst, SPAN), 0:kv_width] = (
            acc_ref[pl.ds(src, SPAN), 0:kv_width] * INV_ROOT
        ).astype(jnp.bfloat16)
        dkv_ref[pl.ds(dst, SPAN), kv_width:] = acc_ref[pl.ds(src, SPAN), kv_width:].astype(
            jnp.bfloat16
        )
        return 0

    lax.fori_loop(0, num_spans, to_layout, 0)


def attention(queries, cotangent, kv_all, doc_list, span_list, rank_index):
    tokens, width = queries.shape
    seq_len, kv_width = kv_all.shape
    chunks = seq_len // CHUNK
    own_spans = lax.dynamic_slice_in_dim(span_list, rank_index * CPR, CPR)
    own_pos = own_spans[:, None] * SPAN + jnp.arange(SPAN, dtype=jnp.int32)[None, :]
    own_docs = doc_list.reshape(-1, SPAN)[own_spans]
    own_start = jnp.sum(
        (doc_list[None, None, :] < own_docs[:, :, None]).astype(jnp.int32), axis=2
    )
    first = own_start[:, 0] // CHUNK
    last = own_spans * SPAN // CHUNK + 1
    bounds = jnp.stack([first, last], axis=1).reshape(-1)
    vmem = pl.BlockSpec(memory_space=pltpu.VMEM)
    smem = pl.BlockSpec(memory_space=pltpu.SMEM)
    return pl.pallas_call(
        attention_kernel,
        out_shape=(
            jax.ShapeDtypeStruct((tokens, width), jnp.bfloat16),
            jax.ShapeDtypeStruct((tokens, width), jnp.bfloat16),
            jax.ShapeDtypeStruct((seq_len, kv_width), jnp.bfloat16),
        ),
        in_specs=[smem, smem, vmem, vmem, vmem, vmem, vmem],
        out_specs=(vmem, vmem, vmem),
        scratch_shapes=[
            pltpu.VMEM((seq_len, kv_width), jnp.bfloat16),
            pltpu.VMEM((seq_len, kv_width), jnp.float32),
            pltpu.VMEM((KVH, chunks, CHUNK, ROWS), jnp.float32),
            pltpu.VMEM((KVH, chunks, CHUNK, ROWS), jnp.bfloat16),
            pltpu.VMEM((KVH, HD, ROWS), jnp.float32),
        ],
        compiler_params=pltpu.CompilerParams(vmem_limit_bytes=52 * 1024 * 1024),
        cost_estimate=pl.CostEstimate(
            flops=12 * tokens * HQ * HD * seq_len // 2,
            bytes_accessed=8 * tokens * width + 4 * seq_len * kv_width,
            transcendentals=tokens * HQ * seq_len,
        ),
        name="attention",
    )(
        span_list,
        bounds,
        queries,
        cotangent,
        kv_all,
        jnp.tile(own_start, (1, GROUP)),
        jnp.tile(own_pos, (1, GROUP)),
    )


def per_device(hidden, queries, keys, cotangent, value_weight, doc_ids, span_order):
    kv_width = keys.shape[2]
    rank_index = lax.axis_index("ctx")
    token_rows = hidden[0]
    weight_all = lax.all_gather(value_weight, "ctx", axis=0, tiled=True)
    features = lax.all_to_all(token_rows, "ctx", split_axis=1, concat_axis=0, tiled=True)
    values_own = jnp.dot(
        token_rows, weight_all, preferred_element_type=jnp.float32
    ).astype(jnp.bfloat16)
    kv_all = lax.all_gather(
        jnp.concatenate([keys[0], values_own], axis=1), "ctx", axis=0, tiled=True
    )
    attention_out, query_grads, kv_terms = attention(
        queries[0], cotangent[0], kv_all, doc_ids[0], span_order[0], rank_index
    )
    kv_own = lax.psum_scatter(kv_terms, "ctx", scatter_dimension=0, tiled=True)
    key_own, value_own = kv_own[:, :kv_width], kv_own[:, kv_width:]
    value_all = lax.all_gather(value_own, "ctx", axis=0, tiled=True)
    input_grads = lax.dot_general(
        value_own, weight_all, NT, preferred_element_type=jnp.float32
    ).astype(jnp.bfloat16)
    weight_part = lax.dot_general(features, value_all, TN, preferred_element_type=jnp.float32)
    weight_total = lax.psum(weight_part.astype(jnp.bfloat16), "dp").astype(jnp.float32)
    weight_grads = (weight_total / lax.axis_size("dp")).astype(jnp.bfloat16)
    return (
        attention_out[None],
        query_grads[None],
        key_own[None],
        input_grads[None],
        weight_grads,
    )


def solution(mesh):
    return jax.shard_map(
        per_device,
        mesh=mesh,
        in_specs=(
            P("dp", "ctx", None),
            P("dp", "ctx", None),
            P("dp", "ctx", None),
            P("dp", "ctx", None),
            P("ctx", None),
            P("dp", None),
            P("dp", None),
        ),
        out_specs=(
            P("dp", "ctx", None),
            P("dp", "ctx", None),
            P("dp", "ctx", None),
            P("dp", "ctx", None),
            P("ctx", None),
        ),
        check_vma=False,
    )
```

profile of v0, /device:TPU:8, one launch (start us, length us, event | category | flops | bytes accessed | tf_op | source)
XLA Modules:
  0.0 411.1 jit_solution(5331198383928662899)
XLA Ops:
  7.3 0.7 all-gather.4.cloned.1.call-update
  8.0 51.2 %all-gather.4.cloned.1.call-done = bf16[4096,512]{1,0:T(8,128)(2,1)} async-done(((bf16[256,512]{1,0:T(8,128)(2,1)}), bf16[4096,512]{1,0:T(8,128)(2,1)}) %all-gather.4.cloned.1.call-update) | async-done | bytes 4194320 | tf_op jit(solution)/shard_map/all_gather | solution.py:211
  59.2 3.2 convolution_convert_fusion.2
  62.4 0.7 pad_maximum_fusion
  63.3 0.1 copy.30
  63.6 0.5 broadcast.154
  64.1 0.7 reduce.5
  64.8 0.1 fusion.3
  64.9 0.6 gather_fusion
  65.5 0.3 convert_reduce_fusion
  66.0 0.1 tile.9.start_ref
  66.0 41.0 %all-gather.6.cloned.1.call-done.kv_ref = bf16[2048,1024]{1,0:T(8,128)(2,1)} async-done(((bf16[128,1024]{1,0:T(8,128)(2,1)}), bf16[2048,1024]{1,0:T(8,128)(2,1)}) %all-gather.6.cloned.1.call-update) | async-done | bytes 4194320 | tf_op jit(solution)/shard_map/all_gather | solution.py:216
  107.1 14.3 %attention.1 = (bf16[128,2048]{1,0:T(8,128)(2,1)}, bf16[128,2048]{1,0:T(8,128)(2,1)}, bf16[2048,1024]{1,0:T(8,128)(2,1)}) custom-call(s32[32]{0:T(128)S(1)} %bitcast.27, s32[4]{0:T(128)S(1)} %reshape.139.bounds_ref, bf16[128,2048]{1,0:T(8,128)(2,1)S(1)} %bitcast.28, bf16[128,2048]{1,0:T(8,128)(2,1)S(1)} %bitcast.29, ...), custom_call_target="tpu_custom_call" | custom-call | flops 3221225472 | bytes 10485760 | tf_op jit(solution)/shard_map/attention/pallas_call | solution.py:173
  121.4 68.6 %reduce-scatter.2.cloned.1.call-done = bf16[128,1024]{1,0:T(8,128)(2,1)} async-done(((bf16[2048,1024]{1,0:T(8,128)(2,1)}), bf16[128,1024]{1,0:T(8,128)(2,1)}) %reduce-scatter.2.cloned.1.call-update) | async-done | bytes 262160 | tf_op jit(solution)/shard_map/reduce_scatter | solution.py:222
  190.0 1.7 fusion.7
  191.8 0.7 copy.34
  192.4 37.9 %all_to_all.19 = bf16[128,16,256]{0,2,1:T(8,128)(2,1)S(1)} all-to-all(bf16[128,16,256]{0,2,1:T(8,128)(2,1)S(1)} %bitcast.32), channel_id=1, replica_groups=mesh['dp'=32,'ctx'=16] {'ctx'}, dimensions={1} | all-to-all | bytes 2097152 | tf_op jit(solution)/shard_map/all_to_all | solution.py:212
  230.4 0.5 copy.35
  230.9 12.9 %all-gather.8.cloned.1.call-done = bf16[2048,512]{1,0:T(8,128)(2,1)} async-done(((bf16[128,512]{1,0:T(8,128)(2,1)}), bf16[2048,512]{1,0:T(8,128)(2,1)}) %all-gather.8.cloned.1.call-update) | async-done | bytes 2097168 | tf_op jit(solution)/shard_map/all_gather | solution.py:224
  243.8 3.1 fusion.1
  246.9 4.6 %fusion = bf16[1,128,4096]{2,1,0:T(8,128)(2,1)} fusion(bf16[4096,512]{1,0:T(8,128)(2,1)} %all-gather.4.cloned.1.call-done, bf16[128,1024]{1,0:T(8,128)(2,1)S(1)} %copy-done.4), kind=kOutput, calls=%fused_computation.2 | convolution fusion | flops 537395200 | bytes 5373952 | tf_op jit(solution)/shard_map/dot_general | solution.py:225
  251.5 151.2 %all-reduce.2.cloned.1.call-done = bf16[256,512]{0,1:T(8,128)(2,1)} async-done(((bf16[256,512]{0,1:T(8,128)(2,1)}), bf16[256,512]{0,1:T(8,128)(2,1)}) %all-reduce.2.cloned.1.call-update) | async-done | bytes 262160 | tf_op jit(solution)/shard_map/psum | solution.py:229
  402.7 1.0 multiply_convert_fusion
  403.7 0.8 copy.36
  (33 shorter events, 0.8 us)
Async XLA Ops:
  7.2 55.2 %copy-start.5 = (bf16[1,128,512]{2,1,0:T(8,128)(2,1)S(1)}, bf16[1,128,512]{2,1,0:T(8,128)(2,1)}, u32[]{:S(2)}) copy-start(bf16[1,128,512]{2,1,0:T(8,128)(2,1)} %param.9) | copy-start | bytes 393220
  7.2 56.0 %copy-start = (s32[1,32]{1,0:T(1,128)S(1)}, s32[1,32]{1,0:T(1,128)}, u32[]{:S(2)}) copy-start(s32[1,32]{1,0:T(1,128)} %param.13) | copy-start | bytes 388
  7.2 56.9 %copy-start.6 = (s32[1,2048]{1,0:T(1,128)S(1)}, s32[1,2048]{1,0:T(1,128)}, u32[]{:S(2)}) copy-start(s32[1,2048]{1,0:T(1,128)} %param.12) | copy-start | bytes 24580
  7.2 99.9 %copy-start.2 = (bf16[1,128,2048]{2,1,0:T(8,128)(2,1)S(1)}, bf16[1,128,2048]{2,1,0:T(8,128)(2,1)}, u32[]{:S(2)}) copy-start(bf16[1,128,2048]{2,1,0:T(8,128)(2,1)} %param.10) | copy-start | bytes 1572868
  7.2 99.9 %copy-start.1 = (bf16[1,128,2048]{2,1,0:T(8,128)(2,1)S(1)}, bf16[1,128,2048]{2,1,0:T(8,128)(2,1)}, u32[]{:S(2)}) copy-start(bf16[1,128,2048]{2,1,0:T(8,128)(2,1)} %param.8) | copy-start | bytes 1572868
  7.2 51.9 %all-gather.4.cloned.1.call-start = ((), (), s32[]{:S(2)}) async-start(), calls=%async_computation.2 | async-start | bytes 4456448 | tf_op jit(solution)/shard_map/all_gather | solution.py:211
  8.0 99.1 %all-gather.6.cloned.1.call-start = ((), (), s32[]{:S(2)}) async-start(), calls=%async_computation.3 | async-start | bytes 4456448 | tf_op jit(solution)/shard_map/all_gather | solution.py:216
  63.2 126.8 %reduce-scatter.2.cloned.1.call-start = ((), (), s32[]{:S(2)}) async-start(), calls=%async_computation.4 | async-start | bytes 4456448 | tf_op jit(solution)/shard_map/reduce_scatter | solution.py:222
  121.4 70.4 %copy-start.3 = (bf16[1,128,4096]{2,1,0:T(8,128)(2,1)S(1)}, bf16[1,128,4096]{2,1,0:T(8,128)(2,1)}, u32[]{:S(2)}) copy-start(bf16[1,128,4096]{2,1,0:T(8,128)(2,1)} %param.7) | copy-start | bytes 3145732
  121.4 122.4 %all-gather.8.cloned.1.call-start = ((), (), s32[]{:S(2)}) async-start(), calls=%async_computation.5 | async-start | bytes 2228224 | tf_op jit(solution)/shard_map/all_gather | solution.py:224
  191.7 211.0 %all-reduce.2.cloned.1.call-start = ((), (), s32[]{:S(2)}) async-start(), calls=%async_computation.6 | async-start | bytes 524288 | tf_op jit(solution)/shard_map/psum | solution.py:229
  192.4 54.4 %copy-start.4 = (bf16[128,1024]{1,0:T(8,128)(2,1)S(1)}, bf16[128,1024]{1,0:T(8,128)(2,1)}, u32[]{:S(2)}) copy-start(bf16[128,1024]{1,0:T(8,128)(2,1)} %reduce-scatter.2.cloned.1.call-done) | copy-start | bytes 786436
Sparse Core Ops, SparseCore 0:
  10.2 48.9 all-gather.3
  63.3 43.7 all-gather.5
  121.5 68.4 reduce-scatter.1
  192.5 51.1 all-gather.7
  247.7 155.0 all-reduce.1
where the time goes:
time: 411 us
  waiting for transfers between devices  326 us (79%)
  blocking collectives  37.9 us (9%)
  Pallas kernels  14.3 us (3%)
  between operations  13.9 us (3%)
  matrix products  10.9 us (3%)
  local copies, waits for them, and re-layouts  5.24 us (1%)
    psum x1, waiting for transfers between devices, per_device(): lax.psum(weight_part.astype(jnp.bfloat16), 'dp').astype(jnp.float32)  151 us
    reduce_scatter x1, waiting for transfers between devices, per_device(): kv_own = lax.psum_scatter(kv_terms, 'ctx', scatter_dimension=0, tiled=True)  68.6 us
    all_gather x1, waiting for transfers between devices, per_device(): weight_all = lax.all_gather(value_weight, 'ctx', axis=0, tiled=True)  51.2 us
    all_gather x1, waiting for transfers between devices, per_device(): lax.all_gather(jnp.concatenate([keys[0], values_own], axis=1), 'ctx', axi...  41 us
    all_to_all x1, blocking collectives, per_device(): lax.all_to_all(token_rows, 'ctx', split_axis=1, concat_axis=0, tiled=True)  37.9 us
    pallas_call x1, Pallas kernels, attention(): pl.pallas_call(attention_kernel, out_shape=(jax.ShapeDtypeStruct((tokens,...  14.3 us
    all_gather x1, waiting for transfers between devices, per_device(): value_all = lax.all_gather(value_own, 'ctx', axis=0, tiled=True)  12.9 us
  transfers between devices with their start and end apart: 5, of which 5 were waited for; matrix products, arithmetic and copies ran while one was open for 2% of the time, Pallas kernels for 0%

commit v1 on v0

--- a/solution.py
+++ b/solution.py
@@ -1,3 +1,4 @@
+import functools
 import math
 
 import jax
@@ -18,6 +19,11 @@
 INV_ROOT = 1.0 / math.sqrt(HD)
 LOG2_SCALE = INV_ROOT * math.log2(math.e)
 FAR = -1e30
+RING = 8
+N_Z = 8
+N_X = 4
+STEPS = RING // 2
+MESH = pl.DeviceIdType.MESH
 
 NT = (((1,), (1,)), ((), ()))
 TN = (((0,), (0,)), ((), ()))
@@ -33,7 +39,8 @@
     bounds_ref,
     q_ref,
     do_ref,
-    kv_ref,
+    k_ref,
+    v_ref,
     start_ref,
     pos_ref,
     o_ref,
@@ -51,7 +58,8 @@
     def to_sequence(i, _):
         src = pl.multiple_of(i * SPAN, SPAN)
         dst = pl.multiple_of(spans_ref[i] * SPAN, SPAN)
-        seq_ref[pl.ds(dst, SPAN), :] = kv_ref[pl.ds(src, SPAN), :]
+        seq_ref[pl.ds(dst, SPAN), 0:kv_width] = k_ref[pl.ds(src, SPAN), :]
+        seq_ref[pl.ds(dst, SPAN), kv_width:] = v_ref[pl.ds(src, SPAN), :]
         acc_ref[pl.ds(src, SPAN), :] = jnp.zeros((SPAN, 2 * kv_width), jnp.float32)
         return 0
 
@@ -155,9 +163,10 @@
     lax.fori_loop(0, num_spans, to_layout, 0)
 
 
-def attention(queries, cotangent, kv_all, doc_list, span_list, rank_index):
+def attention(queries, cotangent, k_all, v_all, doc_list, span_list, rank_index):
     tokens, width = queries.shape
-    seq_len, kv_width = kv_all.shape
+    seq_len = k_all.shape[0]
+    kv_width = 2 * k_all.shape[1]
     chunks = seq_len // CHUNK
     own_spans = lax.dynamic_slice_in_dim(span_list, rank_index * CPR, CPR)
     own_pos = own_spans[:, None] * SPAN + jnp.arange(SPAN, dtype=jnp.int32)[None, :]
@@ -177,7 +186,7 @@
             jax.ShapeDtypeStruct((tokens, width), jnp.bfloat16),
             jax.ShapeDtypeStruct((seq_len, kv_width), jnp.bfloat16),
         ),
-        in_specs=[smem, smem, vmem, vmem, vmem, vmem, vmem],
+        in_specs=[smem, smem, vmem, vmem, vmem, vmem, vmem, vmem],
         out_specs=(vmem, vmem, vmem),
         scratch_shapes=[
             pltpu.VMEM((seq_len, kv_width), jnp.bfloat16),
@@ -198,36 +207,427 @@
         bounds,
         queries,
         cotangent,
-        kv_all,
+        k_all,
+        v_all,
         jnp.tile(own_start, (1, GROUP)),
         jnp.tile(own_pos, (1, GROUP)),
     )
+
+
+def ring_place():
+    me = lax.axis_index("ctx")
+    y, core = me // 2, me % 2
+
+    def at(chip, which):
+        return {"ctx": lax.rem(chip + RING, RING) * 2 + which}
+
+    return y, core, at(y + 1, core), at(y - 1, core), at(y, 1 - core)
+
+
+def greet(partners):
+    barrier = pltpu.get_barrier_semaphore()
+    for partner in partners:
+        pl.semaphore_signal(barrier, inc=1, device_id=partner, device_id_type=MESH)
+    pl.semaphore_wait(barrier, len(partners))
+
+
+def push(src, dst, send_sem, recv_sem, target):
+    return pltpu.make_async_remote_copy(
+        src_ref=src,
+        dst_ref=dst,
+        send_sem=send_sem,
+        recv_sem=recv_sem,
+        device_id=target,
+        device_id_type=MESH,
+    )
+
+
+def carried(direction, step, half, short_step):
+    return step != short_step or half == direction
+
+
+def gather_kernel(count, *refs):
+    in_refs, out_refs = refs[:count], refs[count : 2 * count]
+    local_sem, ring_send, ring_recv, own_send, own_recv, sib_send, sib_recv = refs[2 * count :]
+    y, core, right, left, sibling = ring_place()
+    greet((right, left, sibling))
+
+    def piece(a, chip, which, half):
+        rows = in_refs[a].shape[0] // 2
+        start = (lax.rem(chip + RING, RING) * 4 + which * 2 + half) * rows
+        return out_refs[a].at[pl.ds(pl.multiple_of(start, rows), rows), :]
+
+    def block(a, chip, which):
+        rows = in_refs[a].shape[0]
+        start = (lax.rem(chip + RING, RING) * 2 + which) * rows
+        return out_refs[a].at[pl.ds(pl.multiple_of(start, rows), rows), :]
+
+    sent = []
+    local = []
+    for a in range(count):
+        half_rows = in_refs[a].shape[0] // 2
+        for direction, target in ((0, right), (1, left)):
+            for half in range(2):
+                copy = push(
+                    in_refs[a].at[pl.ds(half * half_rows, half_rows), :],
+                    piece(a, y, core, half),
+                    ring_send.at[a, direction, 0, half],
+                    ring_recv.at[a, direction, 0, half],
+                    target,
+                )
+                copy.start()
+                sent.append(copy)
+    for a in range(count):
+        copy = push(in_refs[a], block(a, y, core), own_send.at[a], own_recv.at[a], sibling)
+        copy.start()
+        sent.append(copy)
+        copy = pltpu.make_async_copy(in_refs[a], block(a, y, core), local_sem.at[a])
+        copy.start()
+        local.append(copy)
+    for step in range(STEPS):
+        for a in range(count):
+            for half in range(2):
+                for direction, target in ((0, right), (1, left)):
+                    if not carried(direction, step, half, STEPS - 1):
+                        continue
+                    chip = y - 1 - step if direction == 0 else y + 1 + step
+                    here = piece(a, chip, core, half)
+                    push(
+                        here,
+                        here,
+                        ring_send.at[a, direction, step, half],
+                        ring_recv.at[a, direction, step, half],
+                        target,
+                    ).wait_recv()
+                    if step + 1 < STEPS and carried(direction, step + 1, half, STEPS - 1):
+                        copy = push(
+                            here,
+                            here,
+                            ring_send.at[a, direction, step + 1, half],
+                            ring_recv.at[a, direction, step + 1, half],
+                            target,
+                        )
+                        copy.start()
+                        sent.append(copy)
+                    copy = push(
+                        here,
+                        here,
+                        sib_send.at[a, direction, step, half],
+                        sib_recv.at[a, direction, step, half],
+                        sibling,
+                    )
+                    copy.start()
+                    sent.append(copy)
+    for a in range(count):
+        there = block(a, y, 1 - core)
+        push(there, there, own_send.at[a], own_recv.at[a], sibling).wait_recv()
+        for step in range(STEPS):
+            for half in range(2):
+                for direction in range(2):
+                    if not carried(direction, step, half, STEPS - 1):
+                        continue
+                    chip = y - 1 - step if direction == 0 else y + 1 + step
+                    there = piece(a, chip, 1 - core, half)
+                    push(
+                        there,
+                        there,
+                        sib_send.at[a, direction, step, half],
+                        sib_recv.at[a, direction, step, half],
+                        sibling,
+                    ).wait_recv()
+    for copy in local:
+        copy.wait()
+    for copy in sent:
+        copy.wait_send()
+
+
+def gather(arrays, collective_id, name):
+    count = len(arrays)
+    ring = pltpu.SemaphoreType.DMA((count, 2, STEPS, 2))
+    one = pltpu.SemaphoreType.DMA((count,))
+    anywhere = pl.BlockSpec(memory_space=pl.ANY)
+    total = sum(a.size for a in arrays) * 2 * RING
+    return pl.pallas_call(
+        functools.partial(gather_kernel, count),
+        out_shape=tuple(
+            jax.ShapeDtypeStruct((a.shape[0] * 2 * RING, a.shape[1]), a.dtype) for a in arrays
+        ),
+        in_specs=[anywhere] * count,
+        out_specs=(anywhere,) * count,
+        scratch_shapes=[one, ring, ring, one, one, ring, ring],
+        compiler_params=pltpu.CompilerParams(collective_id=collective_id, has_side_effects=True),
+        cost_estimate=pl.CostEstimate(flops=0, bytes_accessed=4 * total, transcendentals=0),
+        name=name,
+    )(*arrays)
+
+
+NEAR = (4, 3, -3, 2, -2, 1, -1, 0)
+
+
+def ring_reduce(x_ref, sib_ref, send_ref, recv_ref, sems, place, finish):
+    sib_send, sib_recv, ring_send, ring_recv = sems
+    y, core, right, left, sibling = place
+    rows = sib_ref.shape[1]
+    half_rows = rows // 2
+    sent = []
+    waited = set()
+
+    def row_start(offset, which):
+        return (lax.rem(y + offset + RING, RING) * 2 + which) * rows
+
+    for i, offset in enumerate(NEAR):
+        start = pl.multiple_of(row_start(offset, 1 - core), rows)
+        copy = push(
+            x_ref.at[pl.ds(start, rows), :],
+            sib_ref.at[i],
+            sib_send.at[i],
+            sib_recv.at[i],
+            sibling,
+        )
+        copy.start()
+        sent.append(copy)
+
+    def term(offset, half):
+        i = NEAR.index(4 if offset == -4 else offset)
+        if i not in waited:
+            waited.add(i)
+            push(
+                sib_ref.at[i], sib_ref.at[i], sib_send.at[i], sib_recv.at[i], sibling
+            ).wait_recv()
+        start = pl.multiple_of(row_start(offset, core) + half * half_rows, half_rows)
+        mine = x_ref[pl.ds(start, half_rows), :].astype(jnp.float32)
+        theirs = sib_ref[i, half * half_rows : (half + 1) * half_rows, :]
+        return mine + theirs.astype(jnp.float32)
+
+    def arrived(direction, step, half):
+        slot = recv_ref.at[direction, step, half]
+        push(
+            slot,
+            slot,
+            ring_send.at[direction, step, half],
+            ring_recv.at[direction, step, half],
+            right if direction == 0 else left,
+        ).wait_recv()
+        return recv_ref[direction, step, half].astype(jnp.float32)
+
+    for step in range(STEPS):
+        for half in range(2):
+            for direction, target in ((0, right), (1, left)):
+                if not carried(direction, step, half, 0):
+                    continue
+                distance = STEPS - step
+                value = term(distance if direction == 0 else -distance, half)
+                if step > 0 and carried(direction, step - 1, half, 0):
+                    value = value + arrived(direction, step - 1, half)
+                send_ref[direction, step, half] = value.astype(jnp.bfloat16)
+                copy = push(
+                    send_ref.at[direction, step, half],
+                    recv_ref.at[direction, step, half],
+                    ring_send.at[direction, step, half],
+                    ring_recv.at[direction, step, half],
+                    target,
+                )
+                copy.start()
+                sent.append(copy)
+    for half in range(2):
+        value = term(0, half) + arrived(0, STEPS - 1, half) + arrived(1, STEPS - 1, half)
+        finish(half, value)
+    return sent
+
+
+def ring_scratch(rows, cols):
+    slots = pltpu.VMEM((2, STEPS, 2, rows // 2, cols), jnp.bfloat16)
+    ring = pltpu.SemaphoreType.DMA((2, STEPS, 2))
+    return [
+        pltpu.VMEM((RING, rows, cols), jnp.bfloat16),
+        slots,
+        slots,
+        pltpu.SemaphoreType.DMA((RING,)),
+        pltpu.SemaphoreType.DMA((RING,)),
+        ring,
+        ring,
+    ]
+
+
+def scatter_kernel(x_ref, out_ref, sib_ref, send_ref, recv_ref, *sems):
+    place = ring_place()
+    greet(place[2:])
+    half_rows = out_ref.shape[0] // 2
+
+    def finish(half, value):
+        out_ref[half * half_rows : (half + 1) * half_rows, :] = value.astype(jnp.bfloat16)
+
+    for copy in ring_reduce(x_ref, sib_ref, send_ref, recv_ref, sems, place, finish):
+        copy.wait_send()
+
+
+def reduce_scatter(x, collective_id, name):
+    rows, cols = x.shape[0] // (2 * RING), x.shape[1]
+    vmem = pl.BlockSpec(memory_space=pltpu.VMEM)
+    return pl.pallas_call(
+        scatter_kernel,
+        out_shape=jax.ShapeDtypeStruct((rows, cols), x.dtype),
+        in_specs=[vmem],
+        out_specs=vmem,
+        scratch_shapes=ring_scratch(rows, cols),
+        compiler_params=pltpu.CompilerParams(
+            collective_id=collective_id,
+            has_side_effects=True,
+            vmem_limit_bytes=40 * 1024 * 1024,
+        ),
+        cost_estimate=pl.CostEstimate(
+            flops=4 * x.size, bytes_accessed=4 * x.size, transcendentals=0
+        ),
+        name=name,
+    )(x)
+
+
+def weight_kernel(
+    x_ref,
+    out_ref,
+    sib_ref,
+    send_ref,
+    recv_ref,
+    sib_send,
+    sib_recv,
+    ring_send,
+    ring_recv,
+    own_ref,
+    z_ref,
+    part_ref,
+    x_slots,
+    total_ref,
+    z_send,
+    z_recv,
+    x_send,
+    x_recv,
+    g_send,
+    g_recv,
+):
+    place = ring_place()
+    dp = lax.axis_index("dp")
+    z, x = dp // N_X, dp % N_X
+    z_after = [{"dp": lax.rem(z + k, N_Z) * N_X + x} for k in range(1, N_Z)]
+    x_after = [{"dp": z * N_X + lax.rem(x + k, N_X)} for k in range(1, N_X)]
+    greet(tuple(place[2:]) + tuple(z_after) + tuple(x_after))
+    half_rows = own_ref.shape[0] // 2
+    rows = own_ref.shape[0] // N_Z
+
+    def finish(half, value):
+        own_ref[half * half_rows : (half + 1) * half_rows, :] = value.astype(jnp.bfloat16)
+
+    def z_rows(owner):
+        return pl.ds(pl.multiple_of(lax.rem(owner + N_Z, N_Z) * rows, rows), rows)
+
+    sems = (sib_send, sib_recv, ring_send, ring_recv)
+    sent = ring_reduce(x_ref, sib_ref, send_ref, recv_ref, sems, place, finish)
+    copies = [
+        push(
+            own_ref.at[z_rows(z + k), :],
+            z_ref.at[k - 1],
+            z_send.at[k - 1],
+            z_recv.at[k - 1],
+            z_after[k - 1],
+        )
+        for k in range(1, N_Z)
+    ]
+    for copy in copies:
+        copy.start()
+    sent += copies
+    total = own_ref[z_rows(z), :].astype(jnp.float32)
+    for k in range(1, N_Z):
+        copies[k - 1].wait_recv()
+        total = total + z_ref[k - 1].astype(jnp.float32)
+    part_ref[...] = total.astype(jnp.bfloat16)
+    x_slots[x] = part_ref[...]
+    copies = [
+        push(part_ref, x_slots.at[x], x_send.at[k - 1], x_recv.at[k - 1], x_after[k - 1])
+        for k in range(1, N_X)
+    ]
+    for copy in copies:
+        copy.start()
+    sent += copies
+    for k in range(1, N_X):
+        slot = x_slots.at[lax.rem(x - k + N_X, N_X)]
+        push(slot, slot, x_send.at[k - 1], x_recv.at[k - 1], x_after[k - 1]).wait_recv()
+    total = x_slots[0].astype(jnp.float32)
+    for k in range(1, N_X):
+        total = total + x_slots[k].astype(jnp.float32)
+    total_ref[z_rows(z), :] = (total * (1.0 / (N_Z * N_X))).astype(jnp.bfloat16)
+    here = total_ref.at[z_rows(z), :]
+    copies = [
+        push(here, here, g_send.at[k - 1], g_recv.at[k - 1], z_after[k - 1])
+        for k in range(1, N_Z)
+    ]
+    for copy in copies:
+        copy.start()
+    sent += copies
+    for k in range(1, N_Z):
+        there = total_ref.at[z_rows(z - k), :]
+        push(there, there, g_send.at[k - 1], g_recv.at[k - 1], z_after[k - 1]).wait_recv()
+    out_ref[...] = total_ref[...]
+    for copy in sent:
+        copy.wait_send()
+
+
+def reduce_weights(x, collective_id, name):
+    rows, cols = x.shape[0] // (2 * RING), x.shape[1]
+    part = rows // N_Z
+    vmem = pl.BlockSpec(memory_space=pltpu.VMEM)
+    z_sem = pltpu.SemaphoreType.DMA((N_Z - 1,))
+    x_sem = pltpu.SemaphoreType.DMA((N_X - 1,))
+    return pl.pallas_call(
+        weight_kernel,
+        out_shape=jax.ShapeDtypeStruct((rows, cols), x.dtype),
+        in_specs=[vmem],
+        out_specs=vmem,
+        scratch_shapes=ring_scratch(rows, cols)
+        + [
+            pltpu.VMEM((rows, cols), jnp.bfloat16),
+            pltpu.VMEM((N_Z - 1, part, cols), jnp.bfloat16),
+            pltpu.VMEM((part, cols), jnp.bfloat16),
+            pltpu.VMEM((N_X, part, cols), jnp.bfloat16),
+            pltpu.VMEM((rows, cols), jnp.bfloat16),
+            z_sem,
+            z_sem,
+            x_sem,
+            x_sem,
+            z_sem,
+            z_sem,
+        ],
+        compiler_params=pltpu.CompilerParams(
+            collective_id=collective_id,
+            has_side_effects=True,
+            vmem_limit_bytes=40 * 1024 * 1024,
+        ),
+        cost_estimate=pl.CostEstimate(
+            flops=4 * x.size, bytes_accessed=4 * x.size, transcendentals=0
+        ),
+        name=name,
+    )(x)
 
 
 def per_device(hidden, queries, keys, cotangent, value_weight, doc_ids, span_order):
     kv_width = keys.shape[2]
     rank_index = lax.axis_index("ctx")
     token_rows = hidden[0]
-    weight_all = lax.all_gather(value_weight, "ctx", axis=0, tiled=True)
-    features = lax.all_to_all(token_rows, "ctx", split_axis=1, concat_axis=0, tiled=True)
+    weight_all, key_all = gather((value_weight, keys[0]), 0, "gather_weight_keys")
     values_own = jnp.dot(
         token_rows, weight_all, preferred_element_type=jnp.float32
     ).astype(jnp.bfloat16)
-    kv_all = lax.all_gather(
-        jnp.concatenate([keys[0], values_own], axis=1), "ctx", axis=0, tiled=True
+    (value_all,) = gather((values_own,), 1, "gather_values")
+    attention_out, query_grads, kv_terms = attention(
+        queries[0], cotangent[0], key_all, value_all, doc_ids[0], span_order[0], rank_index
     )
-    attention_out, query_grads, kv_terms = attention(
-        queries[0], cotangent[0], kv_all, doc_ids[0], span_order[0], rank_index
-    )
-    kv_own = lax.psum_scatter(kv_terms, "ctx", scatter_dimension=0, tiled=True)
+    kv_own = reduce_scatter(kv_terms, 2, "scatter_terms")
     key_own, value_own = kv_own[:, :kv_width], kv_own[:, kv_width:]
-    value_all = lax.all_gather(value_own, "ctx", axis=0, tiled=True)
+    weight_part = lax.dot_general(
+        token_rows, value_own, TN, preferred_element_type=jnp.float32
+    ).astype(jnp.bfloat16)
+    weight_grads = reduce_weights(weight_part, 3, "reduce_weights")
     input_grads = lax.dot_general(
         value_own, weight_all, NT, preferred_element_type=jnp.float32
     ).astype(jnp.bfloat16)
-    weight_part = lax.dot_general(features, value_all, TN, preferred_element_type=jnp.float32)
-    weight_total = lax.psum(weight_part.astype(jnp.bfloat16), "dp").astype(jnp.float32)
-    weight_grads = (weight_total / lax.axis_size("dp")).astype(jnp.bfloat16)
     return (
         attention_out[None],
         query_grads[None],

time: 411 us -> 189 us (0.46)
  the two profiles are of different devices: /device:TPU:8 before, /device:TPU:24 now
where the time goes in v1:
time: 189 us; the launch traced here: 188 us
  Pallas kernels  172 us (91%)
  matrix products  7.31 us (4%)
  local copies, waits for them, and re-layouts  5.07 us (3%)
  other arithmetic  3.48 us (2%)
    pallas_call x1, Pallas kernels, reduce_weights(): pl.pallas_call(weight_kernel, out_shape=jax.ShapeDtypeStruct((rows, cols)...  64.5 us
    pallas_call x2, Pallas kernels, gather(): pl.pallas_call(functools.partial(gather_kernel, count), out_shape=tuple((...  60.6 us
    pallas_call x1, Pallas kernels, reduce_scatter(): pl.pallas_call(scatter_kernel, out_shape=jax.ShapeDtypeStruct((rows, cols...  33.9 us
    pallas_call x1, Pallas kernels, attention(): pl.pallas_call(attention_kernel, out_shape=(jax.ShapeDtypeStruct((tokens,...  12.6 us

profile of v1, /device:TPU:24, one launch (start us, length us, event | category | flops | bytes accessed | tf_op | source)
XLA Modules:
  0.0 188.2 jit_solution(15895799797562660295)
XLA Ops:
  0.7 0.9 multiply_bitcast_fusion
  1.6 0.1 iota_add_fusion
  1.6 0.1 copy.22
  1.7 0.1 fusion.7
  1.8 0.1 tile.21.pos_ref
  1.9 0.5 broadcast.153
  2.4 1.4 reduce.5
  3.8 0.1 reshape_squeeze.3
  3.9 0.6 gather_fusion
  4.4 1.0 convert_reduce_fusion
  5.4 0.1 pad_add_fusion
  5.5 0.1 reshape.135.bounds_ref
  5.6 0.1 tile.9.start_ref
  5.7 38.9 %gather_weight_keys.1 = (bf16[4096,512]{1,0:T(8,128)(2,1)}, bf16[2048,512]{1,0:T(8,128)(2,1)}) custom-call(bf16[256,512]{1,0:T(8,128)(2,1)} %refs_0_.1, bf16[128,512]{1,0:T(8,128)(2,1)} %bitcast.29), custom_call_target="tpu_custom_call" | custom-call | bytes 12582912 | tf_op jit(solution)/shard_map/gather_weight_keys/pallas_call | solution.py:350
  44.6 3.6 %fusion.2.refs_0_ = bf16[128,512]{1,0:T(8,128)(2,1)} fusion(bf16[4096,512]{1,0:T(8,128)(2,1)} %get-tuple-element.11, bf16[1,128,4096]{2,1,0:T(8,128)(2,1)S(1)} %copy-done), kind=kOutput, calls=%fused_computation.6 | convolution fusion | flops 536936448 | bytes 5373952 | tf_op jit(solution)/shard_map/dot_general | solution.py:615
  48.1 21.7 %gather_values.1.v_ref = bf16[2048,512]{1,0:T(8,128)(2,1)} custom-call(bf16[128,512]{1,0:T(8,128)(2,1)} %fusion.2.refs_0_), custom_call_target="tpu_custom_call" | custom-call | bytes 4194304 | tf_op jit(solution)/shard_map/gather_values/pallas_call | solution.py:350
  69.9 12.6 %attention.1 = (bf16[128,2048]{1,0:T(8,128)(2,1)}, bf16[128,2048]{1,0:T(8,128)(2,1)}, bf16[2048,1024]{1,0:T(8,128)(2,1)}) custom-call(s32[32]{0:T(128)S(1)} %bitcast.26, s32[4]{0:T(128)S(1)} %reshape.135.bounds_ref, bf16[128,2048]{1,0:T(8,128)(2,1)S(1)} %bitcast.27, bf16[128,2048]{1,0:T(8,128)(2,1)S(1)} %bitcast.28, ...), custom_call_target="tpu_custom_call" | custom-call | flops 3221225472 | bytes 10485760 | tf_op jit(solution)/shard_map/attention/pallas_call | solution.py:182
  82.5 2.2 %copy-done.1 = bf16[2048,1024]{1,0:T(8,128)(2,1)S(1)} copy-done((bf16[2048,1024]{1,0:T(8,128)(2,1)S(1)}, bf16[2048,1024]{1,0:T(8,128)(2,1)}, u32[]{:S(2)}) %copy-start.1) | copy-done | bytes 4194328
  84.7 33.9 %scatter_terms.1 = bf16[128,1024]{1,0:T(8,128)(2,1)S(1)} custom-call(bf16[2048,1024]{1,0:T(8,128)(2,1)S(1)} %copy-done.1), custom_call_target="tpu_custom_call" | custom-call | flops 8388608 | bytes 8388608 | tf_op jit(solution)/shard_map/scatter_terms/pallas_call | solution.py:467
  118.6 2.5 %fusion.1 = bf16[1,128,4096]{2,1,0:T(8,128)(2,1)} fusion(bf16[4096,512]{1,0:T(8,128)(2,1)S(1)} %copy-done.5, bf16[128,1024]{1,0:T(8,128)(2,1)S(1)} %scatter_terms.1), kind=kOutput, calls=%fused_computation.4 | convolution fusion | flops 537395200 | bytes 5373952 | tf_op jit(solution)/shard_map/dot_general | solution.py:628
  121.0 0.7 slice_bitcast_fusion
  121.7 1.3 fusion.x_ref
  123.0 64.5 %reduce_weights.1 = bf16[256,512]{1,0:T(8,128)(2,1)S(1)} custom-call(bf16[4096,512]{1,0:T(8,128)(2,1)S(1)} %fusion.x_ref), custom_call_target="tpu_custom_call" | custom-call | flops 8388608 | bytes 8388608 | tf_op jit(solution)/shard_map/reduce_weights/pallas_call | solution.py:579
  187.5 0.7 copy.31
  (15 shorter events, 0.0 us)
Async XLA Ops:
  0.6 43.9 %copy-start = (bf16[1,128,4096]{2,1,0:T(8,128)(2,1)S(1)}, bf16[1,128,4096]{2,1,0:T(8,128)(2,1)}, u32[]{:S(2)}) copy-start(bf16[1,128,4096]{2,1,0:T(8,128)(2,1)} %param.7) | copy-start | bytes 3145732
  0.6 69.2 %copy-start.2 = (s32[1,32]{1,0:T(1,128)S(1)}, s32[1,32]{1,0:T(1,128)}, u32[]{:S(2)}) copy-start(s32[1,32]{1,0:T(1,128)} %param.13) | copy-start | bytes 388
  0.7 69.2 %copy-start.4 = (bf16[1,128,2048]{2,1,0:T(8,128)(2,1)S(1)}, bf16[1,128,2048]{2,1,0:T(8,128)(2,1)}, u32[]{:S(2)}) copy-start(bf16[1,128,2048]{2,1,0:T(8,128)(2,1)} %param.10) | copy-start | bytes 1572868
  0.7 69.2 %copy-start.3 = (bf16[1,128,2048]{2,1,0:T(8,128)(2,1)S(1)}, bf16[1,128,2048]{2,1,0:T(8,128)(2,1)}, u32[]{:S(2)}) copy-start(bf16[1,128,2048]{2,1,0:T(8,128)(2,1)} %param.8) | copy-start | bytes 1572868
  69.9 48.7 %copy-start.5 = (bf16[4096,512]{1,0:T(8,128)(2,1)S(1)}, bf16[4096,512]{1,0:T(8,128)(2,1)}, u32[]{:S(2)}) copy-start(bf16[4096,512]{1,0:T(8,128)(2,1)} %get-tuple-element.11) | copy-start | bytes 12582916
  82.5 2.2 %copy-start.1 = (bf16[2048,1024]{1,0:T(8,128)(2,1)S(1)}, bf16[2048,1024]{1,0:T(8,128)(2,1)}, u32[]{:S(2)}) copy-start(bf16[2048,1024]{1,0:T(8,128)(2,1)} %get-tuple-element.14.x_ref) | copy-start | bytes 12582916

commit v2 on v1

--- a/solution.py
+++ b/solution.py
@@ -36,13 +36,12 @@
 
 def attention_kernel(
     spans_ref,
-    bounds_ref,
+    rank_ref,
+    docs_ref,
     q_ref,
     do_ref,
     k_ref,
     v_ref,
-    start_ref,
-    pos_ref,
     o_ref,
     dq_ref,
     dkv_ref,
@@ -90,11 +89,31 @@
     def value_cols(head):
         return slice(kv_width + head * HD, kv_width + (head + 1) * HD)
 
+    def first_with(doc, low, high, rounds):
+        def halve(_, ends):
+            low, high = ends
+            mid = (low + high) // 2
+            below = docs_ref[mid] < doc
+            return jnp.where(below, mid + 1, low), jnp.where(below, high, mid)
+
+        return lax.fori_loop(0, rounds, halve, (low, high))[1]
+
     for span in range(CPR):
-        first = bounds_ref[2 * span]
-        last = bounds_ref[2 * span + 1]
-        start = start_ref[span : span + 1, :]
-        pos = pos_ref[span : span + 1, :]
+        begin = spans_ref[rank_ref[0] * CPR + span] * SPAN
+        doc_low = docs_ref[begin]
+        doc_high = docs_ref[begin + SPAN - 1]
+        pos = begin + lax.broadcasted_iota(jnp.int32, (1, ROWS), 1) % SPAN
+        lowest = first_with(doc_low, 0, begin, 11)
+        first = lowest // CHUNK
+        last = begin // CHUNK + 1
+
+        def next_doc(doc, start):
+            bound = first_with(doc, begin, begin + SPAN - 1, 6)
+            return jnp.where(pos >= bound, bound, start)
+
+        start = lax.fori_loop(
+            doc_low + 1, doc_high + 1, next_doc, jnp.full((1, ROWS), lowest, jnp.int32)
+        )
 
         def score_step(c, carry):
             rows = pl.ds(pl.multiple_of(c * CHUNK, CHUNK), CHUNK)
@@ -168,15 +187,6 @@
     seq_len = k_all.shape[0]
     kv_width = 2 * k_all.shape[1]
     chunks = seq_len // CHUNK
-    own_spans = lax.dynamic_slice_in_dim(span_list, rank_index * CPR, CPR)
-    own_pos = own_spans[:, None] * SPAN + jnp.arange(SPAN, dtype=jnp.int32)[None, :]
-    own_docs = doc_list.reshape(-1, SPAN)[own_spans]
-    own_start = jnp.sum(
-        (doc_list[None, None, :] < own_docs[:, :, None]).astype(jnp.int32), axis=2
-    )
-    first = own_start[:, 0] // CHUNK
-    last = own_spans * SPAN // CHUNK + 1
-    bounds = jnp.stack([first, last], axis=1).reshape(-1)
     vmem = pl.BlockSpec(memory_space=pltpu.VMEM)
     smem = pl.BlockSpec(memory_space=pltpu.SMEM)
     return pl.pallas_call(
@@ -186,7 +196,7 @@
             jax.ShapeDtypeStruct((tokens, width), jnp.bfloat16),
             jax.ShapeDtypeStruct((seq_len, kv_width), jnp.bfloat16),
         ),
-        in_specs=[smem, smem, vmem, vmem, vmem, vmem, vmem, vmem],
+        in_specs=[smem, smem, smem, vmem, vmem, vmem, vmem],
         out_specs=(vmem, vmem, vmem),
         scratch_shapes=[
             pltpu.VMEM((seq_len, kv_width), jnp.bfloat16),
@@ -204,13 +214,12 @@
         name="attention",
     )(
         span_list,
-        bounds,
+        jnp.reshape(rank_index, (1,)),
+        doc_list,
         queries,
         cotangent,
         k_all,
         v_all,
-        jnp.tile(own_start, (1, GROUP)),
-        jnp.tile(own_pos, (1, GROUP)),
     )
 
 
@@ -246,119 +255,204 @@
     return step != short_step or half == direction
 
 
-def gather_kernel(count, *refs):
-    in_refs, out_refs = refs[:count], refs[count : 2 * count]
-    local_sem, ring_send, ring_recv, own_send, own_recv, sib_send, sib_recv = refs[2 * count :]
-    y, core, right, left, sibling = ring_place()
-    greet((right, left, sibling))
-
-    def piece(a, chip, which, half):
-        rows = in_refs[a].shape[0] // 2
+class RingGather:
+    def __init__(self, a, own_ref, all_ref, sems, place):
+        self.a, self.own_ref, self.all_ref = a, own_ref, all_ref
+        self.rows = own_ref.shape[0]
+        (
+            self.local_sem,
+            self.ring_send,
+            self.ring_recv,
+            self.own_send,
+            self.own_recv,
+            self.sib_send,
+            self.sib_recv,
+        ) = sems
+        self.y, self.core, self.right, self.left, self.sibling = place
+        self.sent = []
+
+    def piece(self, chip, which, half):
+        rows = self.rows // 2
         start = (lax.rem(chip + RING, RING) * 4 + which * 2 + half) * rows
-        return out_refs[a].at[pl.ds(pl.multiple_of(start, rows), rows), :]
-
-    def block(a, chip, which):
-        rows = in_refs[a].shape[0]
-        start = (lax.rem(chip + RING, RING) * 2 + which) * rows
-        return out_refs[a].at[pl.ds(pl.multiple_of(start, rows), rows), :]
-
-    sent = []
-    local = []
-    for a in range(count):
-        half_rows = in_refs[a].shape[0] // 2
-        for direction, target in ((0, right), (1, left)):
-            for half in range(2):
-                copy = push(
-                    in_refs[a].at[pl.ds(half * half_rows, half_rows), :],
-                    piece(a, y, core, half),
-                    ring_send.at[a, direction, 0, half],
-                    ring_recv.at[a, direction, 0, half],
-                    target,
-                )
-                copy.start()
-                sent.append(copy)
-    for a in range(count):
-        copy = push(in_refs[a], block(a, y, core), own_send.at[a], own_recv.at[a], sibling)
+        return self.all_ref.at[pl.ds(pl.multiple_of(start, rows), rows), :]
+
+    def block(self, chip, which):
+        start = (lax.rem(chip + RING, RING) * 2 + which) * self.rows
+        return self.all_ref.at[pl.ds(pl.multiple_of(start, self.rows), self.rows), :]
+
+    def send(self, copy):
         copy.start()
-        sent.append(copy)
-        copy = pltpu.make_async_copy(in_refs[a], block(a, y, core), local_sem.at[a])
-        copy.start()
-        local.append(copy)
+        self.sent.append(copy)
+
+    def along(self, src, dst, direction, step, half):
+        return push(
+            src,
+            dst,
+            self.ring_send.at[self.a, direction, step, half],
+            self.ring_recv.at[self.a, direction, step, half],
+            self.left if direction else self.right,
+        )
+
+    def across(self, ref, direction, step, half):
+        return push(
+            ref,
+            ref,
+            self.sib_send.at[self.a, direction, step, half],
+            self.sib_recv.at[self.a, direction, step, half],
+            self.sibling,
+        )
+
+    def own_across(self, src, dst):
+        return push(src, dst, self.own_send.at[self.a], self.own_recv.at[self.a], self.sibling)
+
+    def start(self):
+        rows = self.rows // 2
+        for half in range(2):
+            for direction in range(2):
+                src = self.own_ref.at[pl.ds(half * rows, rows), :]
+                dst = self.piece(self.y, self.core, half)
+                self.send(self.along(src, dst, direction, 0, half))
+        mine = self.block(self.y, self.core)
+        self.send(self.own_across(self.own_ref, mine))
+        self.local = pltpu.make_async_copy(self.own_ref, mine, self.local_sem.at[self.a])
+        self.local.start()
+
+    def pieces(self, step):
+        for half in range(2):
+            for direction in range(2):
+                if carried(direction, step, half, STEPS - 1):
+                    chip = self.y + 1 + step if direction else self.y - 1 - step
+                    yield direction, half, chip
+
+    def step(self, step):
+        for direction, half, chip in self.pieces(step):
+            here = self.piece(chip, self.core, half)
+            self.along(here, here, direction, step, half).wait_recv()
+            if step + 1 < STEPS and carried(direction, step + 1, half, STEPS - 1):
+                self.send(self.along(here, here, direction, step + 1, half))
+            self.send(self.across(here, direction, step, half))
+
+    def own_from_sibling(self):
+        there = self.block(self.y, 1 - self.core)
+        self.own_across(there, there).wait_recv()
+
+    def from_sibling(self, step):
+        for direction, half, chip in self.pieces(step):
+            there = self.piece(chip, 1 - self.core, half)
+            self.across(there, direction, step, half).wait_recv()
+
+    def finish(self):
+        self.local.wait()
+        for copy in self.sent:
+            copy.wait_send()
+
+
+def front_kernel(
+    hidden_ref,
+    weight_ref,
+    keys_ref,
+    weight_out,
+    key_out,
+    value_out,
+    weight_all,
+    acc_ref,
+    values_ref,
+    out_sem,
+    *sems,
+):
+    place = ring_place()
+    y, core = place[:2]
+    greet(place[2:])
+    weight = RingGather(0, weight_ref, weight_all, sems, place)
+    key = RingGather(1, keys_ref, key_out, sems, place)
+    value = RingGather(2, values_ref, value_out, sems, place)
+    depth = weight_ref.shape[0]
+
+    def project(chip, which):
+        start = (lax.rem(chip + RING, RING) * 2 + which) * depth
+        rows = pl.ds(pl.multiple_of(start, depth), depth)
+        acc_ref[...] += mm(hidden_ref[:, rows], weight_all[rows, :], NN)
+
+    weight.start()
+    acc_ref[...] = jnp.zeros_like(acc_ref)
     for step in range(STEPS):
-        for a in range(count):
-            for half in range(2):
-                for direction, target in ((0, right), (1, left)):
-                    if not carried(direction, step, half, STEPS - 1):
-                        continue
-                    chip = y - 1 - step if direction == 0 else y + 1 + step
-                    here = piece(a, chip, core, half)
-                    push(
-                        here,
-                        here,
-                        ring_send.at[a, direction, step, half],
-                        ring_recv.at[a, direction, step, half],
-                        target,
-                    ).wait_recv()
-                    if step + 1 < STEPS and carried(direction, step + 1, half, STEPS - 1):
-                        copy = push(
-                            here,
-                            here,
-                            ring_send.at[a, direction, step + 1, half],
-                            ring_recv.at[a, direction, step + 1, half],
-                            target,
-                        )
-                        copy.start()
-                        sent.append(copy)
-                    copy = push(
-                        here,
-                        here,
-                        sib_send.at[a, direction, step, half],
-                        sib_recv.at[a, direction, step, half],
-                        sibling,
-                    )
-                    copy.start()
-                    sent.append(copy)
-    for a in range(count):
-        there = block(a, y, 1 - core)
-        push(there, there, own_send.at[a], own_recv.at[a], sibling).wait_recv()
+        weight.step(step)
+        if step == STEPS - 2:
+            key.start()
+        if step == 0:
+            weight.local.wait()
+            project(y, core)
+            weight.own_from_sibling()
+            project(y, 1 - core)
+        else:
+            weight.from_sibling(step - 1)
+            project(y - step, 1 - core)
+            project(y + step, 1 - core)
+        project(y - 1 - step, core)
+        if step < STEPS - 1:
+            project(y + 1 + step, core)
+    weight.from_sibling(STEPS - 1)
+    project(y + STEPS, 1 - core)
+    values_ref[...] = acc_ref[...].astype(jnp.bfloat16)
+    value.start()
+    keep = pltpu.make_async_copy(weight_all, weight_out, out_sem)
+    keep.start()
+    for step in range(STEPS):
+        key.step(step)
+        value.step(step)
+    for each in (key, value):
+        each.own_from_sibling()
         for step in range(STEPS):
-            for half in range(2):
-                for direction in range(2):
-                    if not carried(direction, step, half, STEPS - 1):
-                        continue
-                    chip = y - 1 - step if direction == 0 else y + 1 + step
-                    there = piece(a, chip, 1 - core, half)
-                    push(
-                        there,
-                        there,
-                        sib_send.at[a, direction, step, half],
-                        sib_recv.at[a, direction, step, half],
-                        sibling,
-                    ).wait_recv()
-    for copy in local:
-        copy.wait()
-    for copy in sent:
+            each.from_sibling(step)
+    keep.wait()
+    for each in (key, value):
+        each.finish()
+    for copy in weight.sent:
         copy.wait_send()
 
 
-def gather(arrays, collective_id, name):
-    count = len(arrays)
-    ring = pltpu.SemaphoreType.DMA((count, 2, STEPS, 2))
-    one = pltpu.SemaphoreType.DMA((count,))
+def front(hidden, value_weight, keys, collective_id):
+    tokens, kv_width = keys.shape
+    ring = pltpu.SemaphoreType.DMA((3, 2, STEPS, 2))
+    one = pltpu.SemaphoreType.DMA((3,))
     anywhere = pl.BlockSpec(memory_space=pl.ANY)
-    total = sum(a.size for a in arrays) * 2 * RING
+    vmem = pl.BlockSpec(memory_space=pltpu.VMEM)
+    depth = value_weight.shape[0] * 2 * RING
+    gathered = jax.ShapeDtypeStruct((tokens * 2 * RING, kv_width), keys.dtype)
     return pl.pallas_call(
-        functools.partial(gather_kernel, count),
-        out_shape=tuple(
-            jax.ShapeDtypeStruct((a.shape[0] * 2 * RING, a.shape[1]), a.dtype) for a in arrays
-        ),
-        in_specs=[anywhere] * count,
-        out_specs=(anywhere,) * count,
-        scratch_shapes=[one, ring, ring, one, one, ring, ring],
-        compiler_params=pltpu.CompilerParams(collective_id=collective_id, has_side_effects=True),
-        cost_estimate=pl.CostEstimate(flops=0, bytes_accessed=4 * total, transcendentals=0),
-        name=name,
-    )(*arrays)
+        front_kernel,
+        out_shape=(
+            jax.ShapeDtypeStruct((depth, kv_width), value_weight.dtype),
+            gathered,
+            gathered,
+        ),
+        in_specs=[vmem, vmem, vmem],
+        out_specs=(anywhere,) * 3,
+        scratch_shapes=[
+            pltpu.VMEM((depth, kv_width), jnp.bfloat16),
+            pltpu.VMEM((tokens, kv_width), jnp.float32),
+            pltpu.VMEM((tokens, kv_width), jnp.bfloat16),
+            pltpu.SemaphoreType.DMA,
+            one,
+            ring,
+            ring,
+            one,
+            one,
+            ring,
+            ring,
+        ],
+        compiler_params=pltpu.CompilerParams(
+            collective_id=collective_id,
+            has_side_effects=True,
+            vmem_limit_bytes=24 * 1024 * 1024,
+        ),
+        cost_estimate=pl.CostEstimate(
+            flops=2 * tokens * depth * kv_width,
+            bytes_accessed=4 * depth * kv_width,
+            transcendentals=0,
+        ),
+        name="front",
+    )(hidden, value_weight, keys)
 
 
 NEAR = (4, 3, -3, 2, -2, 1, -1, 0)
@@ -611,11 +705,7 @@
     kv_width = keys.shape[2]
     rank_index = lax.axis_index("ctx")
     token_rows = hidden[0]
-    weight_all, key_all = gather((value_weight, keys[0]), 0, "gather_weight_keys")
-    values_own = jnp.dot(
-        token_rows, weight_all, preferred_element_type=jnp.float32
-    ).astype(jnp.bfloat16)
-    (value_all,) = gather((values_own,), 1, "gather_values")
+    weight_all, key_all, value_all = front(token_rows, value_weight, keys[0], 0)
     attention_out, query_grads, kv_terms = attention(
         queries[0], cotangent[0], key_all, value_all, doc_ids[0], span_order[0], rank_index
     )

time: 189 us -> 180 us (0.952)
  Pallas kernels: 172 us -> 162 us
  local copies, waits for them, and re-layouts: 5.07 us -> 12.7 us
  matrix products: 7.31 us -> 3.74 us
  other arithmetic: 3.48 us -> 0 us
    unnamed x14 -> x23, local copies, waits for them, and re-layouts: 3.43 us -> 12 us
    pallas_call x2 -> x1, Pallas kernels: 60.6 us -> 52.4 us  [front(): pl.pallas_call(front_kernel, out_shape=(jax.ShapeDtypeStruct((depth, kv_w...]
    dot_general x1 -> x0, matrix products: 3.56 us -> none  [per_device(): jnp.dot(token_rows, weight_all, preferred_element_type=jnp.float32)]
    pallas_call x1, Pallas kernels: 33.9 us -> 31.6 us  [reduce_scatter(): pl.pallas_call(scatter_kernel, out_shape=jax.ShapeDtypeStruct((rows, cols...]
    pallas_call x1, Pallas kernels: 12.6 us -> 14.6 us  [attention(): pl.pallas_call(attention_kernel, out_shape=(jax.ShapeDtypeStruct((tokens,...]
where the time goes in v2:
time: 180 us; the launch traced here: 179 us
  Pallas kernels  162 us (90%)
  local copies, waits for them, and re-layouts  12.7 us (7%)
  matrix products  3.74 us (2%)
    pallas_call x1, Pallas kernels, reduce_weights(): pl.pallas_call(weight_kernel, out_shape=jax.ShapeDtypeStruct((rows, cols)...  63.6 us
    pallas_call x1, Pallas kernels, front(): pl.pallas_call(front_kernel, out_shape=(jax.ShapeDtypeStruct((depth, kv_w...  52.4 us
    pallas_call x1, Pallas kernels, reduce_scatter(): pl.pallas_call(scatter_kernel, out_shape=jax.ShapeDtypeStruct((rows, cols...  31.6 us
    pallas_call x1, Pallas kernels, attention(): pl.pallas_call(attention_kernel, out_shape=(jax.ShapeDtypeStruct((tokens,...  14.6 us
    unnamed x23, local copies, waits for them, and re-layouts  12 us

profile of v2, /device:TPU:24, one launch (start us, length us, event | category | flops | bytes accessed | tf_op | source)
XLA Modules:
  0.0 179.4 jit_solution(6773708085466659695)
XLA Ops:
  0.6 0.0 copy-start.1
  0.6 1.2 copy-done.1
  1.9 0.0 copy-start.5
  1.9 0.9 copy-done.5
  2.8 0.0 copy-start.6
  2.8 0.9 copy-done.6
  3.7 52.4 %front.1 = (bf16[4096,512]{1,0:T(8,128)(2,1)S(1)}, bf16[2048,512]{1,0:T(8,128)(2,1)S(1)}, bf16[2048,512]{1,0:T(8,128)(2,1)S(1)}) custom-call(bf16[128,4096]{1,0:T(8,128)(2,1)S(1)} %bitcast.18, bf16[256,512]{1,0:T(8,128)(2,1)S(1)} %copy-done.5, bf16[128,512]{1,0:T(8,128)(2,1)S(1)} %bitcast.21), custom_call_target="tpu_custom_call" | custom-call | flops 536870912 | bytes 8388608 | tf_op jit(solution)/shard_map/front/pallas_call | solution.py:422
  56.1 0.0 copy-start.9
  56.1 1.3 copy-done.9
  57.4 0.0 copy-start.10
  57.4 1.3 copy-done.10
  58.7 1.0 copy-done.3
  59.8 1.0 copy-done.4
  60.8 0.7 copy-done.7
  61.5 0.7 copy-done.8
  62.2 14.6 %attention.1 = (bf16[128,2048]{1,0:T(8,128)(2,1)}, bf16[128,2048]{1,0:T(8,128)(2,1)}, bf16[2048,1024]{1,0:T(8,128)(2,1)}) custom-call(s32[32]{0:T(128)S(1)} %bitcast.23, s32[1]{0:T(128)} %bitcast.1.rank_ref, s32[2048]{0:T(1024)S(1)} %bitcast.22, bf16[128,2048]{1,0:T(8,128)(2,1)S(1)} %bitcast.19, bf16[128,2048]{1,0:T(8,128)(2,1)S(1)} %bitcast.20, ...), custom_call_target="tpu_custom_call" | custom-call | flops 3221225472 | bytes 10485760 | tf_op jit(solution)/shard_map/attention/pallas_call | solution.py:192
  76.8 2.2 %copy-done = bf16[2048,1024]{1,0:T(8,128)(2,1)S(1)} copy-done((bf16[2048,1024]{1,0:T(8,128)(2,1)S(1)}, bf16[2048,1024]{1,0:T(8,128)(2,1)}, u32[]{:S(2)}) %copy-start) | copy-done | bytes 4194328
  79.0 31.6 %scatter_terms.1 = bf16[128,1024]{1,0:T(8,128)(2,1)S(1)} custom-call(bf16[2048,1024]{1,0:T(8,128)(2,1)S(1)} %copy-done), custom_call_target="tpu_custom_call" | custom-call | flops 8388608 | bytes 8388608 | tf_op jit(solution)/shard_map/scatter_terms/pallas_call | solution.py:561
  110.6 2.5 %fusion.1 = bf16[1,128,4096]{2,1,0:T(8,128)(2,1)} fusion(bf16[4096,512]{1,0:T(8,128)(2,1)S(1)} %get-tuple-element.16, bf16[128,1024]{1,0:T(8,128)(2,1)S(1)} %scatter_terms.1), kind=kOutput, calls=%fused_computation.3 | convolution fusion | flops 537395200 | bytes 5373952 | tf_op jit(solution)/shard_map/dot_general | solution.py:718
  113.0 0.7 slice_bitcast_fusion
  113.7 0.0 copy-done.2
  113.7 1.3 fusion.x_ref
  115.0 63.6 %reduce_weights.1 = bf16[256,512]{1,0:T(8,128)(2,1)S(1)} custom-call(bf16[4096,512]{1,0:T(8,128)(2,1)S(1)} %fusion.x_ref), custom_call_target="tpu_custom_call" | custom-call | flops 8388608 | bytes 8388608 | tf_op jit(solution)/shard_map/reduce_weights/pallas_call | solution.py:673
  178.6 0.7 copy.15
  (6 shorter events, 0.0 us)
Async XLA Ops:
  0.6 1.2 copy-start.1
  1.9 0.9 copy-start.5
  2.8 0.9 copy-start.6
  56.1 1.3 copy-start.9
  57.4 1.3 copy-start.10
  58.7 1.0 copy-start.3
  59.8 1.0 copy-start.4
  60.8 0.7 copy-start.7
  61.5 0.7 copy-start.8
  76.8 2.2 %copy-start = (bf16[2048,1024]{1,0:T(8,128)(2,1)S(1)}, bf16[2048,1024]{1,0:T(8,128)(2,1)}, u32[]{:S(2)}) copy-start(bf16[2048,1024]{1,0:T(8,128)(2,1)} %get-tuple-element.15.x_ref) | copy-start | bytes 12582916
  79.0 34.7 %copy-start.2 = (bf16[1,128,4096]{2,1,0:T(8,128)(2,1)S(1)}, bf16[1,128,4096]{2,1,0:T(8,128)(2,1)}, u32[]{:S(2)}) copy-start(bf16[1,128,4096]{2,1,0:T(8,128)(2,1)} %param.7) | copy-start | bytes 3145732

commit v3 on v2

--- a/solution.py
+++ b/solution.py
@@ -205,7 +205,7 @@
             pltpu.VMEM((KVH, chunks, CHUNK, ROWS), jnp.bfloat16),
             pltpu.VMEM((KVH, HD, ROWS), jnp.float32),
         ],
-        compiler_params=pltpu.CompilerParams(vmem_limit_bytes=52 * 1024 * 1024),
+        compiler_params=pltpu.CompilerParams(vmem_limit_bytes=40 * 1024 * 1024),
         cost_estimate=pl.CostEstimate(
             flops=12 * tokens * HQ * HD * seq_len // 2,
             bytes_accessed=8 * tokens * width + 4 * seq_len * kv_width,
@@ -458,139 +458,100 @@
 NEAR = (4, 3, -3, 2, -2, 1, -1, 0)
 
 
-def ring_reduce(x_ref, sib_ref, send_ref, recv_ref, sems, place, finish):
-    sib_send, sib_recv, ring_send, ring_recv = sems
-    y, core, right, left, sibling = place
-    rows = sib_ref.shape[1]
-    half_rows = rows // 2
-    sent = []
-    waited = set()
-
-    def row_start(offset, which):
-        return (lax.rem(y + offset + RING, RING) * 2 + which) * rows
-
-    for i, offset in enumerate(NEAR):
-        start = pl.multiple_of(row_start(offset, 1 - core), rows)
-        copy = push(
-            x_ref.at[pl.ds(start, rows), :],
-            sib_ref.at[i],
-            sib_send.at[i],
-            sib_recv.at[i],
-            sibling,
-        )
-        copy.start()
-        sent.append(copy)
-
-    def term(offset, half):
-        i = NEAR.index(4 if offset == -4 else offset)
-        if i not in waited:
-            waited.add(i)
-            push(
-                sib_ref.at[i], sib_ref.at[i], sib_send.at[i], sib_recv.at[i], sibling
-            ).wait_recv()
-        start = pl.multiple_of(row_start(offset, core) + half * half_rows, half_rows)
-        mine = x_ref[pl.ds(start, half_rows), :].astype(jnp.float32)
-        theirs = sib_ref[i, half * half_rows : (half + 1) * half_rows, :]
-        return mine + theirs.astype(jnp.float32)
-
-    def arrived(direction, step, half):
-        slot = recv_ref.at[direction, step, half]
-        push(
-            slot,
-            slot,
-            ring_send.at[direction, step, half],
-            ring_recv.at[direction, step, half],
-            right if direction == 0 else left,
-        ).wait_recv()
-        return recv_ref[direction, step, half].astype(jnp.float32)
-
-    for step in range(STEPS):
+class RingReduce:
+    def __init__(self, term, send_ref, recv_ref, ring_send, ring_recv, place):
+        self.term, self.send_ref, self.recv_ref = term, send_ref, recv_ref
+        self.ring_send, self.ring_recv = ring_send, ring_recv
+        self.targets = place[2:4]
+        self.sent = []
+
+    def copy(self, src, direction, step, half):
+        return push(
+            src,
+            self.recv_ref.at[direction, step, half],
+            self.ring_send.at[direction, step, half],
+            self.ring_recv.at[direction, step, half],
+            self.targets[direction],
+        )
+
+    def arrived(self, direction, step, half):
+        self.copy(self.send_ref.at[direction, step, half], direction, step, half).wait_recv()
+        return self.recv_ref[direction, step, half].astype(jnp.float32)
+
+    def step(self, step):
+        distance = STEPS - step
         for half in range(2):
-            for direction, target in ((0, right), (1, left)):
+            for direction in range(2):
                 if not carried(direction, step, half, 0):
                     continue
-                distance = STEPS - step
-                value = term(distance if direction == 0 else -distance, half)
+                value = self.term(-distance if direction else distance, half)
                 if step > 0 and carried(direction, step - 1, half, 0):
-                    value = value + arrived(direction, step - 1, half)
-                send_ref[direction, step, half] = value.astype(jnp.bfloat16)
-                copy = push(
-                    send_ref.at[direction, step, half],
-                    recv_ref.at[direction, step, half],
-                    ring_send.at[direction, step, half],
-                    ring_recv.at[direction, step, half],
-                    target,
-                )
+                    value = value + self.arrived(direction, step - 1, half)
+                self.send_ref[direction, step, half] = value.astype(jnp.bfloat16)
+                copy = self.copy(self.send_ref.at[direction, step, half], direction, step, half)
                 copy.start()
-                sent.append(copy)
-    for half in range(2):
-        value = term(0, half) + arrived(0, STEPS - 1, half) + arrived(1, STEPS - 1, half)
-        finish(half, value)
-    return sent
-
-
-def ring_scratch(rows, cols):
-    slots = pltpu.VMEM((2, STEPS, 2, rows // 2, cols), jnp.bfloat16)
-    ring = pltpu.SemaphoreType.DMA((2, STEPS, 2))
-    return [
-        pltpu.VMEM((RING, rows, cols), jnp.bfloat16),
-        slots,
-        slots,
-        pltpu.SemaphoreType.DMA((RING,)),
-        pltpu.SemaphoreType.DMA((RING,)),
-        ring,
-        ring,
-    ]
-
-
-def scatter_kernel(x_ref, out_ref, sib_ref, send_ref, recv_ref, *sems):
-    place = ring_place()
-    greet(place[2:])
-    half_rows = out_ref.shape[0] // 2
-
-    def finish(half, value):
-        out_ref[half * half_rows : (half + 1) * half_rows, :] = value.astype(jnp.bfloat16)
-
-    for copy in ring_reduce(x_ref, sib_ref, send_ref, recv_ref, sems, place, finish):
-        copy.wait_send()
-
-
-def reduce_scatter(x, collective_id, name):
-    rows, cols = x.shape[0] // (2 * RING), x.shape[1]
-    vmem = pl.BlockSpec(memory_space=pltpu.VMEM)
-    return pl.pallas_call(
-        scatter_kernel,
-        out_shape=jax.ShapeDtypeStruct((rows, cols), x.dtype),
-        in_specs=[vmem],
-        out_specs=vmem,
-        scratch_shapes=ring_scratch(rows, cols),
-        compiler_params=pltpu.CompilerParams(
-            collective_id=collective_id,
-            has_side_effects=True,
-            vmem_limit_bytes=40 * 1024 * 1024,
-        ),
-        cost_estimate=pl.CostEstimate(
-            flops=4 * x.size, bytes_accessed=4 * x.size, transcendentals=0
-        ),
-        name=name,
-    )(x)
-
-
-def weight_kernel(
-    x_ref,
-    out_ref,
-    sib_ref,
-    send_ref,
-    recv_ref,
-    sib_send,
-    sib_recv,
-    ring_send,
-    ring_recv,
+                self.sent.append(copy)
+
+    def result(self, half):
+        value = self.term(0, half)
+        for direction in range(2):
+            value = value + self.arrived(direction, STEPS - 1, half)
+        return value
+
+
+class FromSibling:
+    def __init__(self, land_ref, send_sem, recv_sem, sibling):
+        self.land_ref, self.send_sem, self.recv_sem = land_ref, send_sem, recv_sem
+        self.sibling = sibling
+        self.sent = []
+        self.waited = set()
+
+    def copy(self, i, src):
+        return push(
+            src, self.land_ref.at[i], self.send_sem.at[i], self.recv_sem.at[i], self.sibling
+        )
+
+    def send(self, i, src):
+        copy = self.copy(i, src)
+        copy.start()
+        self.sent.append(copy)
+
+    def half_block(self, offset, half):
+        i = NEAR.index(4 if offset == -4 else offset)
+        if i not in self.waited:
+            self.waited.add(i)
+            self.copy(i, self.land_ref.at[i]).wait_recv()
+        rows = self.land_ref.shape[1] // 2
+        return self.land_ref[i, half * rows : (half + 1) * rows, :].astype(jnp.float32)
+
+
+def back_kernel(
+    terms_ref,
+    hidden_ref,
+    key_out,
+    value_out,
+    weight_out,
+    t_land,
+    t_send,
+    t_recv,
+    w_stage,
+    w_land,
+    w_send,
+    w_recv,
+    grads_ref,
     own_ref,
-    z_ref,
+    z_land,
     part_ref,
     x_slots,
     total_ref,
+    t_sib_send,
+    t_sib_recv,
+    t_ring_send,
+    t_ring_recv,
+    w_sib_send,
+    w_sib_recv,
+    w_ring_send,
+    w_ring_recv,
     z_send,
     z_recv,
     x_send,
@@ -599,122 +560,225 @@
     g_recv,
 ):
     place = ring_place()
+    y, core = place[:2]
+    sibling = place[4]
     dp = lax.axis_index("dp")
     z, x = dp // N_X, dp % N_X
     z_after = [{"dp": lax.rem(z + k, N_Z) * N_X + x} for k in range(1, N_Z)]
     x_after = [{"dp": z * N_X + lax.rem(x + k, N_X)} for k in range(1, N_X)]
     greet(tuple(place[2:]) + tuple(z_after) + tuple(x_after))
-    half_rows = own_ref.shape[0] // 2
-    rows = own_ref.shape[0] // N_Z
-
-    def finish(half, value):
-        own_ref[half * half_rows : (half + 1) * half_rows, :] = value.astype(jnp.bfloat16)
-
-    def z_rows(owner):
-        return pl.ds(pl.multiple_of(lax.rem(owner + N_Z, N_Z) * rows, rows), rows)
-
-    sems = (sib_send, sib_recv, ring_send, ring_recv)
-    sent = ring_reduce(x_ref, sib_ref, send_ref, recv_ref, sems, place, finish)
-    copies = [
-        push(
-            own_ref.at[z_rows(z + k), :],
-            z_ref.at[k - 1],
-            z_send.at[k - 1],
-            z_recv.at[k - 1],
+
+    tokens = hidden_ref.shape[0]
+    width = key_out.shape[1]
+    depth = own_ref.shape[0]
+
+    def owner(offset, which):
+        return lax.rem(y + offset + RING, RING) * 2 + which
+
+    def term_sums(n, first_col):
+        cols = slice(first_col, first_col + width)
+        sib = FromSibling(t_land.at[n], t_sib_send.at[n], t_sib_recv.at[n], sibling)
+        for i, offset in enumerate(NEAR):
+            start = pl.multiple_of(owner(offset, 1 - core) * tokens, tokens)
+            sib.send(i, terms_ref.at[pl.ds(start, tokens), cols])
+
+        def term(offset, half):
+            rows = tokens // 2
+            start = pl.multiple_of(owner(offset, core) * tokens + half * rows, rows)
+            mine = terms_ref[pl.ds(start, rows), cols].astype(jnp.float32)
+            return mine + sib.half_block(offset, half)
+
+        ring = RingReduce(
+            term, t_send.at[n], t_recv.at[n], t_ring_send.at[n], t_ring_recv.at[n], place
+        )
+        return ring, sib
+
+    value, value_sib = term_sums(0, width)
+    key, key_sib = term_sums(1, 0)
+    value.step(0)
+    value.step(1)
+    key.step(0)
+    value.step(2)
+    key.step(1)
+    value.step(3)
+    key.step(2)
+    rows = tokens // 2
+    for half in range(2):
+        grads_ref[half * rows : (half + 1) * rows, :] = value.result(half).astype(jnp.bfloat16)
+
+    def partial(offset, which, first_row, count):
+        start = pl.multiple_of(owner(offset, which) * depth + first_row, count)
+        return mm(hidden_ref[:, pl.ds(start, count)], grads_ref[...], TN)
+
+    weight_sib = FromSibling(w_land, w_sib_send, w_sib_recv, sibling)
+
+    def weight_term(offset, half):
+        mine = partial(offset, core, half * (depth // 2), depth // 2)
+        return mine + weight_sib.half_block(offset, half)
+
+    weight = RingReduce(weight_term, w_send, w_recv, w_ring_send, w_ring_recv, place)
+
+    def stage(*order):
+        for i in order:
+            w_stage[i] = partial(NEAR[i], 1 - core, 0, depth).astype(jnp.bfloat16)
+            weight_sib.send(i, w_stage.at[i])
+
+    stage(0, 1, 2)
+    weight.step(0)
+    key.step(3)
+    stage(3, 4)
+    weight.step(1)
+    stage(5, 6, 7)
+    weight.step(2)
+    value_out[...] = grads_ref[...]
+    for half in range(2):
+        key_out[half * rows : (half + 1) * rows, :] = key.result(half).astype(jnp.bfloat16)
+    weight.step(3)
+
+    sent = value.sent + key.sent + weight.sent
+    sent += value_sib.sent + key_sib.sent + weight_sib.sent
+    half_depth = depth // 2
+    part = half_depth // N_Z
+
+    def z_rows(half, who):
+        start = half * half_depth + lax.rem(who + N_Z, N_Z) * part
+        return pl.ds(pl.multiple_of(start, part), part)
+
+    def z_copy(half, k):
+        return push(
+            own_ref.at[z_rows(half, z + k), :],
+            z_land.at[half, k - 1],
+            z_send.at[half, k - 1],
+            z_recv.at[half, k - 1],
             z_after[k - 1],
         )
-        for k in range(1, N_Z)
-    ]
-    for copy in copies:
-        copy.start()
-    sent += copies
-    total = own_ref[z_rows(z), :].astype(jnp.float32)
-    for k in range(1, N_Z):
-        copies[k - 1].wait_recv()
-        total = total + z_ref[k - 1].astype(jnp.float32)
-    part_ref[...] = total.astype(jnp.bfloat16)
-    x_slots[x] = part_ref[...]
-    copies = [
-        push(part_ref, x_slots.at[x], x_send.at[k - 1], x_recv.at[k - 1], x_after[k - 1])
-        for k in range(1, N_X)
-    ]
-    for copy in copies:
-        copy.start()
-    sent += copies
-    for k in range(1, N_X):
-        slot = x_slots.at[lax.rem(x - k + N_X, N_X)]
-        push(slot, slot, x_send.at[k - 1], x_recv.at[k - 1], x_after[k - 1]).wait_recv()
-    total = x_slots[0].astype(jnp.float32)
-    for k in range(1, N_X):
-        total = total + x_slots[k].astype(jnp.float32)
-    total_ref[z_rows(z), :] = (total * (1.0 / (N_Z * N_X))).astype(jnp.bfloat16)
-    here = total_ref.at[z_rows(z), :]
-    copies = [
-        push(here, here, g_send.at[k - 1], g_recv.at[k - 1], z_after[k - 1])
-        for k in range(1, N_Z)
-    ]
-    for copy in copies:
-        copy.start()
-    sent += copies
-    for k in range(1, N_Z):
-        there = total_ref.at[z_rows(z - k), :]
-        push(there, there, g_send.at[k - 1], g_recv.at[k - 1], z_after[k - 1]).wait_recv()
-    out_ref[...] = total_ref[...]
+
+    def x_copy(half, k, who):
+        return push(
+            part_ref.at[half],
+            x_slots.at[half, lax.rem(who + N_X, N_X)],
+            x_send.at[half, k - 1],
+            x_recv.at[half, k - 1],
+            x_after[k - 1],
+        )
+
+    def g_copy(half, k, who):
+        there = total_ref.at[z_rows(half, who), :]
+        return push(
+            there, there, g_send.at[half, k - 1], g_recv.at[half, k - 1], z_after[k - 1]
+        )
+
+    for half in range(2):
+        own_ref[half * half_depth : (half + 1) * half_depth, :] = weight.result(half).astype(
+            jnp.bfloat16
+        )
+        for k in range(1, N_Z):
+            copy = z_copy(half, k)
+            copy.start()
+            sent.append(copy)
+    for half in range(2):
+        total = own_ref[z_rows(half, z), :].astype(jnp.float32)
+        for k in range(1, N_Z):
+            z_copy(half, k).wait_recv()
+            total = total + z_land[half, k - 1].astype(jnp.float32)
+        part_ref[half] = total.astype(jnp.bfloat16)
+        x_slots[half, x] = part_ref[half]
+        for k in range(1, N_X):
+            copy = x_copy(half, k, x)
+            copy.start()
+            sent.append(copy)
+    for half in range(2):
+        for k in range(1, N_X):
+            x_copy(half, k, x - k).wait_recv()
+        total = x_slots[half, 0].astype(jnp.float32)
+        for k in range(1, N_X):
+            total = total + x_slots[half, k].astype(jnp.float32)
+        total_ref[z_rows(half, z), :] = (total * (1.0 / (N_Z * N_X))).astype(jnp.bfloat16)
+        for k in range(1, N_Z):
+            copy = g_copy(half, k, z)
+            copy.start()
+            sent.append(copy)
+    for half in range(2):
+        for k in range(1, N_Z):
+            g_copy(half, k, z - k).wait_recv()
+    weight_out[...] = total_ref[...]
     for copy in sent:
         copy.wait_send()
 
 
-def reduce_weights(x, collective_id, name):
-    rows, cols = x.shape[0] // (2 * RING), x.shape[1]
-    part = rows // N_Z
+def back(terms, hidden, collective_id):
+    tokens, features = hidden.shape
+    width = terms.shape[1] // 2
+    depth = features // (2 * RING)
+    part = depth // 2 // N_Z
     vmem = pl.BlockSpec(memory_space=pltpu.VMEM)
-    z_sem = pltpu.SemaphoreType.DMA((N_Z - 1,))
-    x_sem = pltpu.SemaphoreType.DMA((N_X - 1,))
+
+    def buffer(*shape):
+        return pltpu.VMEM(shape, jnp.bfloat16)
+
+    def dma(*shape):
+        return pltpu.SemaphoreType.DMA(shape)
+
+    t_slots = buffer(2, 2, STEPS, 2, tokens // 2, width)
+    w_slots = buffer(2, STEPS, 2, depth // 2, width)
     return pl.pallas_call(
-        weight_kernel,
-        out_shape=jax.ShapeDtypeStruct((rows, cols), x.dtype),
-        in_specs=[vmem],
-        out_specs=vmem,
-        scratch_shapes=ring_scratch(rows, cols)
-        + [
-            pltpu.VMEM((rows, cols), jnp.bfloat16),
-            pltpu.VMEM((N_Z - 1, part, cols), jnp.bfloat16),
-            pltpu.VMEM((part, cols), jnp.bfloat16),
-            pltpu.VMEM((N_X, part, cols), jnp.bfloat16),
-            pltpu.VMEM((rows, cols), jnp.bfloat16),
-            z_sem,
-            z_sem,
-            x_sem,
-            x_sem,
-            z_sem,
-            z_sem,
+        back_kernel,
+        out_shape=(
+            jax.ShapeDtypeStruct((tokens, width), jnp.bfloat16),
+            jax.ShapeDtypeStruct((tokens, width), jnp.bfloat16),
+            jax.ShapeDtypeStruct((depth, width), jnp.bfloat16),
+        ),
+        in_specs=[vmem, vmem],
+        out_specs=(vmem,) * 3,
+        scratch_shapes=[
+            buffer(2, RING, tokens, width),
+            t_slots,
+            t_slots,
+            buffer(RING, depth, width),
+            buffer(RING, depth, width),
+            w_slots,
+            w_slots,
+            buffer(tokens, width),
+            buffer(depth, width),
+            buffer(2, N_Z - 1, part, width),
+            buffer(2, part, width),
+            buffer(2, N_X, part, width),
+            buffer(depth, width),
+            dma(2, RING),
+            dma(2, RING),
+            dma(2, 2, STEPS, 2),
+            dma(2, 2, STEPS, 2),
+            dma(RING),
+            dma(RING),
+            dma(2, STEPS, 2),
+            dma(2, STEPS, 2),
+            dma(2, N_Z - 1),
+            dma(2, N_Z - 1),
+            dma(2, N_X - 1),
+            dma(2, N_X - 1),
+            dma(2, N_Z - 1),
+            dma(2, N_Z - 1),
         ],
         compiler_params=pltpu.CompilerParams(
             collective_id=collective_id,
             has_side_effects=True,
-            vmem_limit_bytes=40 * 1024 * 1024,
+            vmem_limit_bytes=36 * 1024 * 1024,
         ),
         cost_estimate=pl.CostEstimate(
-            flops=4 * x.size, bytes_accessed=4 * x.size, transcendentals=0
-        ),
-        name=name,
-    )(x)
+            flops=2 * hidden.size * width, bytes_accessed=4 * terms.size, transcendentals=0
+        ),
+        name="back",
+    )(terms, hidden)
 
 
 def per_device(hidden, queries, keys, cotangent, value_weight, doc_ids, span_order):
-    kv_width = keys.shape[2]
     rank_index = lax.axis_index("ctx")
     token_rows = hidden[0]
     weight_all, key_all, value_all = front(token_rows, value_weight, keys[0], 0)
     attention_out, query_grads, kv_terms = attention(
         queries[0], cotangent[0], key_all, value_all, doc_ids[0], span_order[0], rank_index
     )
-    kv_own = reduce_scatter(kv_terms, 2, "scatter_terms")
-    key_own, value_own = kv_own[:, :kv_width], kv_own[:, kv_width:]
-    weight_part = lax.dot_general(
-        token_rows, value_own, TN, preferred_element_type=jnp.float32
-    ).astype(jnp.bfloat16)
-    weight_grads = reduce_weights(weight_part, 3, "reduce_weights")
+    key_own, value_own, weight_grads = back(kv_terms, token_rows, 1)
     input_grads = lax.dot_general(
         value_own, weight_all, NT, preferred_element_type=jnp.float32
     ).astype(jnp.bfloat16)

time: 180 us -> 161 us (0.89)
  Pallas kernels: 162 us -> 149 us
  local copies, waits for them, and re-layouts: 12.7 us -> 7.86 us
    pallas_call x2 -> x1, Pallas kernels: 95.2 us -> 79.4 us  [back(): pl.pallas_call(back_kernel, out_shape=(jax.ShapeDtypeStruct((tokens, widt...]
    unnamed x23 -> x18, local copies, waits for them, and re-layouts: 12 us -> 7.86 us
    pallas_call x1, Pallas kernels: 14.6 us -> 17.1 us  [attention(): pl.pallas_call(attention_kernel, out_shape=(jax.ShapeDtypeStruct((tokens,...]
where the time goes in v3:
time: 161 us; the launch traced here: 160 us
  Pallas kernels  149 us (93%)
  local copies, waits for them, and re-layouts  7.86 us (5%)
  matrix products  2.45 us (2%)
    pallas_call x1, Pallas kernels, back(): pl.pallas_call(back_kernel, out_shape=(jax.ShapeDtypeStruct((tokens, widt...  79.4 us
    pallas_call x1, Pallas kernels, front(): pl.pallas_call(front_kernel, out_shape=(jax.ShapeDtypeStruct((depth, kv_w...  52.4 us
    pallas_call x1, Pallas kernels, attention(): pl.pallas_call(attention_kernel, out_shape=(jax.ShapeDtypeStruct((tokens,...  17.1 us
    unnamed x18, local copies, waits for them, and re-layouts  7.86 us

profile of v3, /device:TPU:24, one launch (start us, length us, event | category | flops | bytes accessed | tf_op | source)
XLA Modules:
  0.0 159.8 jit_solution(13406475871368652678)
XLA Ops:
  0.6 0.0 copy-start
  0.6 1.2 copy-done
  1.9 0.0 copy-start.4
  1.9 0.9 copy-done.4
  2.8 0.0 copy-start.5
  2.8 0.9 copy-done.5
  3.7 52.4 %front.1 = (bf16[4096,512]{1,0:T(8,128)(2,1)S(1)}, bf16[2048,512]{1,0:T(8,128)(2,1)S(1)}, bf16[2048,512]{1,0:T(8,128)(2,1)S(1)}) custom-call(bf16[128,4096]{1,0:T(8,128)(2,1)S(1)} %bitcast.14, bf16[256,512]{1,0:T(8,128)(2,1)S(1)} %copy-done.4, bf16[128,512]{1,0:T(8,128)(2,1)S(1)} %bitcast.19), custom_call_target="tpu_custom_call" | custom-call | flops 536870912 | bytes 8388608 | tf_op jit(solution)/shard_map/front/pallas_call | solution.py:422
  56.1 0.0 copy-start.2
  56.1 1.0 copy-done.2
  57.1 0.0 copy-start.3
  57.1 1.0 copy-done.3
  58.2 0.0 copy-start.6
  58.2 0.7 copy-done.6
  58.9 0.0 copy-start.7
  58.9 0.7 copy-done.7
  59.5 0.0 copy-start.1
  59.5 17.1 %attention.1 = (bf16[128,2048]{1,0:T(8,128)(2,1)}, bf16[128,2048]{1,0:T(8,128)(2,1)}, bf16[2048,1024]{1,0:T(8,128)(2,1)S(1)}) custom-call(s32[32]{0:T(128)S(1)} %bitcast.21, s32[1]{0:T(128)} %bitcast.1.rank_ref, s32[2048]{0:T(1024)S(1)} %bitcast.20, bf16[128,2048]{1,0:T(8,128)(2,1)S(1)} %bitcast.17, bf16[128,2048]{1,0:T(8,128)(2,1)S(1)} %bitcast.18, ...), custom_call_target="tpu_custom_call" | custom-call | flops 3221225472 | bytes 10485760 | tf_op jit(solution)/shard_map/attention/pallas_call | solution.py:192
  76.6 0.0 copy-done.1
  76.6 79.4 %back.1 = (bf16[128,512]{1,0:T(8,128)(2,1)S(1)}, bf16[128,512]{1,0:T(8,128)(2,1)S(1)}, bf16[256,512]{1,0:T(8,128)(2,1)S(1)}) custom-call(bf16[2048,1024]{1,0:T(8,128)(2,1)S(1)} %get-tuple-element.18.terms_ref, bf16[128,4096]{1,0:T(8,128)(2,1)S(1)} %bitcast.15), custom_call_target="tpu_custom_call" | custom-call | flops 536870912 | bytes 8388608 | tf_op jit(solution)/shard_map/back/pallas_call | solution.py:724
  156.0 2.4 %fusion = bf16[1,128,4096]{2,1,0:T(8,128)(2,1)} fusion(bf16[128,512]{1,0:T(8,128)(2,1)S(1)} %get-tuple-element.20, bf16[4096,512]{1,0:T(8,128)(2,1)S(1)} %get-tuple-element.21), kind=kOutput, calls=%fused_computation.1 | convolution fusion | flops 537395200 | bytes 5373952 | tf_op jit(solution)/shard_map/dot_general | solution.py:782
  158.4 0.7 copy.14
  159.1 0.7 copy.15
Async XLA Ops:
  0.6 1.2 copy-start
  1.9 0.9 copy-start.4
  2.8 0.9 copy-start.5
  56.1 1.0 copy-start.2
  57.1 1.0 copy-start.3
  58.2 0.7 copy-start.6
  58.9 0.7 copy-start.7
  59.5 17.1 %copy-start.1 = (bf16[1,128,4096]{2,1,0:T(8,128)(2,1)S(1)}, bf16[1,128,4096]{2,1,0:T(8,128)(2,1)}, u32[]{:S(2)}) copy-start(bf16[1,128,4096]{2,1,0:T(8,128)(2,1)} %param.7) | copy-start | bytes 3145732

commit v4 on v3

--- a/solution.py
+++ b/solution.py
@@ -256,9 +256,10 @@
 
 
 class RingGather:
-    def __init__(self, a, own_ref, all_ref, sems, place):
+    def __init__(self, a, own_ref, all_ref, sems, place, stride=None):
         self.a, self.own_ref, self.all_ref = a, own_ref, all_ref
         self.rows = own_ref.shape[0]
+        self.stride = stride or self.rows
         (
             self.local_sem,
             self.ring_send,
@@ -273,11 +274,11 @@
 
     def piece(self, chip, which, half):
         rows = self.rows // 2
-        start = (lax.rem(chip + RING, RING) * 4 + which * 2 + half) * rows
+        start = (lax.rem(chip + RING, RING) * 2 + which) * self.stride + half * rows
         return self.all_ref.at[pl.ds(pl.multiple_of(start, rows), rows), :]
 
     def block(self, chip, which):
-        start = (lax.rem(chip + RING, RING) * 2 + which) * self.rows
+        start = (lax.rem(chip + RING, RING) * 2 + which) * self.stride
         return self.all_ref.at[pl.ds(pl.multiple_of(start, self.rows), self.rows), :]
 
     def send(self, copy):
@@ -305,7 +306,7 @@
     def own_across(self, src, dst):
         return push(src, dst, self.own_send.at[self.a], self.own_recv.at[self.a], self.sibling)
 
-    def start(self):
+    def start(self, in_place=False):
         rows = self.rows // 2
         for half in range(2):
             for direction in range(2):
@@ -314,8 +315,9 @@
                 self.send(self.along(src, dst, direction, 0, half))
         mine = self.block(self.y, self.core)
         self.send(self.own_across(self.own_ref, mine))
-        self.local = pltpu.make_async_copy(self.own_ref, mine, self.local_sem.at[self.a])
-        self.local.start()
+        if not in_place:
+            self.local = pltpu.make_async_copy(self.own_ref, mine, self.local_sem.at[self.a])
+            self.local.start()
 
     def pieces(self, step):
         for half in range(2):
@@ -355,30 +357,68 @@
     key_out,
     value_out,
     weight_all,
+    high_ref,
     acc_ref,
     values_ref,
     out_sem,
+    thin_local,
+    thin_send,
+    thin_recv,
     *sems,
 ):
     place = ring_place()
-    y, core = place[:2]
-    greet(place[2:])
-    weight = RingGather(0, weight_ref, weight_all, sems, place)
+    y, core, _, _, sibling = place
+    dp = lax.axis_index("dp")
+    z, x = dp // N_X, dp % N_X
+    up = {"dp": lax.rem(z + 1, RING) * N_X + x}
+    down = {"dp": lax.rem(z + RING - 1, RING) * N_X + x}
+    chips = [{"ctx": lax.rem(y + k, RING) * 2 + core} for k in range(1, RING)]
+    greet(tuple(chips) + (sibling, up, down))
+    depth = weight_ref.shape[0]
+    low = depth // 2
+    thin = low // RING
+    high_rows = pl.ds(pl.multiple_of((z * 2 + core) * low, low), low)
+
+    def thin_block(chip):
+        start = (z * 2 + core) * low + lax.rem(chip + RING, RING) * thin
+        return high_ref.at[pl.ds(pl.multiple_of(start, thin), thin), :]
+
+    mine = weight_ref.at[pl.ds(pl.multiple_of(low + z * thin, thin), thin), :]
+
+    def thin_copy(k, dst):
+        return push(mine, dst, thin_send.at[k - 1], thin_recv.at[k - 1], chips[k - 1])
+
+    thin_sent = [thin_copy(k, thin_block(y)) for k in range(1, RING)]
+    for copy in thin_sent:
+        copy.start()
+    keep = pltpu.make_async_copy(mine, thin_block(y), thin_local)
+    keep.start()
+
+    weight = RingGather(
+        0, weight_ref.at[pl.ds(0, low), :], weight_all, sems, place, stride=depth
+    )
+    high = RingGather(
+        3, high_ref.at[high_rows, :], high_ref, sems, (z, core, up, down, sibling)
+    )
     key = RingGather(1, keys_ref, key_out, sems, place)
     value = RingGather(2, values_ref, value_out, sems, place)
-    depth = weight_ref.shape[0]
 
     def project(chip, which):
         start = (lax.rem(chip + RING, RING) * 2 + which) * depth
-        rows = pl.ds(pl.multiple_of(start, depth), depth)
+        rows = pl.ds(pl.multiple_of(start, low), low)
         acc_ref[...] += mm(hidden_ref[:, rows], weight_all[rows, :], NN)
 
     weight.start()
     acc_ref[...] = jnp.zeros_like(acc_ref)
+    keep.wait()
+    for k in range(1, RING):
+        thin_copy(k, thin_block(y - k)).wait_recv()
+    high.start(in_place=True)
     for step in range(STEPS):
         weight.step(step)
-        if step == STEPS - 2:
+        if step == 1:
             key.start()
+        high.step(step)
         if step == 0:
             weight.local.wait()
             project(y, core)
@@ -391,14 +431,29 @@
         project(y - 1 - step, core)
         if step < STEPS - 1:
             project(y + 1 + step, core)
+    key.step(0)
     weight.from_sibling(STEPS - 1)
     project(y + STEPS, 1 - core)
-    values_ref[...] = acc_ref[...].astype(jnp.bfloat16)
+    high.own_from_sibling()
+    for step in range(STEPS):
+        high.from_sibling(step)
+    for block in range(2 * RING):
+        chip, which = block // 2, block % 2
+        for layer in range(RING):
+            src = (layer * 2 + which) * low + chip * thin
+            dst = block * depth + low + layer * thin
+            weight_all[dst : dst + thin, :] = high_ref[src : src + thin, :]
+    total = acc_ref[...]
+    for block in range(2 * RING):
+        rows = slice(block * depth + low, (block + 1) * depth)
+        total = total + mm(hidden_ref[:, rows], weight_all[rows, :], NN)
+    values_ref[...] = total.astype(jnp.bfloat16)
     value.start()
     keep = pltpu.make_async_copy(weight_all, weight_out, out_sem)
     keep.start()
     for step in range(STEPS):
-        key.step(step)
+        if step + 1 < STEPS:
+            key.step(step + 1)
         value.step(step)
     for each in (key, value):
         each.own_from_sibling()
@@ -407,14 +462,15 @@
     keep.wait()
     for each in (key, value):
         each.finish()
-    for copy in weight.sent:
+    for copy in weight.sent + high.sent + thin_sent:
         copy.wait_send()
 
 
 def front(hidden, value_weight, keys, collective_id):
     tokens, kv_width = keys.shape
-    ring = pltpu.SemaphoreType.DMA((3, 2, STEPS, 2))
-    one = pltpu.SemaphoreType.DMA((3,))
+    ring = pltpu.SemaphoreType.DMA((4, 2, STEPS, 2))
+    one = pltpu.SemaphoreType.DMA((4,))
+    thin = pltpu.SemaphoreType.DMA((RING - 1,))
     anywhere = pl.BlockSpec(memory_space=pl.ANY)
     vmem = pl.BlockSpec(memory_space=pltpu.VMEM)
     depth = value_weight.shape[0] * 2 * RING
@@ -430,9 +486,13 @@
         out_specs=(anywhere,) * 3,
         scratch_shapes=[
             pltpu.VMEM((depth, kv_width), jnp.bfloat16),
+            pltpu.VMEM((depth // 2, kv_width), jnp.bfloat16),
             pltpu.VMEM((tokens, kv_width), jnp.float32),
             pltpu.VMEM((tokens, kv_width), jnp.bfloat16),
             pltpu.SemaphoreType.DMA,
+            pltpu.SemaphoreType.DMA,
+            thin,
+            thin,
             one,
             ring,
             ring,

time: 161 us -> 162 us (level)
  the two profiles are of different devices: /device:TPU:24 before, /device:TPU:1 now
where the time goes in v4:
time: 162 us; the launch traced here: 161 us
  Pallas kernels  150 us (93%)
  local copies, waits for them, and re-layouts  7.86 us (5%)
  matrix products  2.45 us (2%)
    pallas_call x1, Pallas kernels, back(): pl.pallas_call(back_kernel, out_shape=(jax.ShapeDtypeStruct((tokens, widt...  69.3 us
    pallas_call x1, Pallas kernels, front(): pl.pallas_call(front_kernel, out_shape=(jax.ShapeDtypeStruct((depth, kv_w...  60.1 us
    pallas_call x1, Pallas kernels, attention(): pl.pallas_call(attention_kernel, out_shape=(jax.ShapeDtypeStruct((tokens,...  20.8 us
    unnamed x18, local copies, waits for them, and re-layouts  7.86 us

profile of v4, /device:TPU:1, one launch (start us, length us, event | category | flops | bytes accessed | tf_op | source)
XLA Modules:
  0.0 161.2 jit_solution(8441058663434397110)
XLA Ops:
  0.6 0.0 copy-start
  0.6 1.2 copy-done
  1.9 0.0 copy-start.4
  1.9 0.9 copy-done.4
  2.8 0.0 copy-start.5
  2.8 0.9 copy-done.5
  3.7 60.1 %front.1 = (bf16[4096,512]{1,0:T(8,128)(2,1)S(1)}, bf16[2048,512]{1,0:T(8,128)(2,1)S(1)}, bf16[2048,512]{1,0:T(8,128)(2,1)S(1)}) custom-call(bf16[128,4096]{1,0:T(8,128)(2,1)S(1)} %bitcast.14, bf16[256,512]{1,0:T(8,128)(2,1)S(1)} %copy-done.4, bf16[128,512]{1,0:T(8,128)(2,1)S(1)} %bitcast.19), custom_call_target="tpu_custom_call" | custom-call | flops 536870912 | bytes 8388608 | tf_op jit(solution)/shard_map/front/pallas_call | solution.py:478
  63.8 0.0 copy-start.2
  63.8 1.0 copy-done.2
  64.9 0.0 copy-start.3
  64.9 1.0 copy-done.3
  65.9 0.0 copy-start.6
  65.9 0.7 copy-done.6
  66.6 0.0 copy-start.7
  66.6 0.7 copy-done.7
  67.2 0.0 copy-start.1
  67.3 20.8 %attention.1 = (bf16[128,2048]{1,0:T(8,128)(2,1)}, bf16[128,2048]{1,0:T(8,128)(2,1)}, bf16[2048,1024]{1,0:T(8,128)(2,1)S(1)}) custom-call(s32[32]{0:T(128)S(1)} %bitcast.21, s32[1]{0:T(128)} %bitcast.1.rank_ref, s32[2048]{0:T(1024)S(1)} %bitcast.20, bf16[128,2048]{1,0:T(8,128)(2,1)S(1)} %bitcast.17, bf16[128,2048]{1,0:T(8,128)(2,1)S(1)} %bitcast.18, ...), custom_call_target="tpu_custom_call" | custom-call | flops 3221225472 | bytes 10485760 | tf_op jit(solution)/shard_map/attention/pallas_call | solution.py:192
  88.1 0.0 copy-done.1
  88.1 69.3 %back.1 = (bf16[128,512]{1,0:T(8,128)(2,1)S(1)}, bf16[128,512]{1,0:T(8,128)(2,1)S(1)}, bf16[256,512]{1,0:T(8,128)(2,1)S(1)}) custom-call(bf16[2048,1024]{1,0:T(8,128)(2,1)S(1)} %get-tuple-element.18.terms_ref, bf16[128,4096]{1,0:T(8,128)(2,1)S(1)} %bitcast.15), custom_call_target="tpu_custom_call" | custom-call | flops 536870912 | bytes 8388608 | tf_op jit(solution)/shard_map/back/pallas_call | solution.py:784
  157.4 2.5 %fusion = bf16[1,128,4096]{2,1,0:T(8,128)(2,1)} fusion(bf16[128,512]{1,0:T(8,128)(2,1)S(1)} %get-tuple-element.20, bf16[4096,512]{1,0:T(8,128)(2,1)S(1)} %get-tuple-element.21), kind=kOutput, calls=%fused_computation.1 | convolution fusion | flops 537395200 | bytes 5373952 | tf_op jit(solution)/shard_map/dot_general | solution.py:842
  159.8 0.7 copy.14
  160.5 0.7 copy.15
Async XLA Ops:
  0.6 1.2 copy-start
  1.9 0.9 copy-start.4
  2.8 0.9 copy-start.5
  63.8 1.0 copy-start.2
  64.9 1.0 copy-start.3
  65.9 0.7 copy-start.6
  66.6 0.7 copy-start.7
  67.2 20.9 %copy-start.1 = (bf16[1,128,4096]{2,1,0:T(8,128)(2,1)S(1)}, bf16[1,128,4096]{2,1,0:T(8,128)(2,1)}, u32[]{:S(2)}) copy-start(bf16[1,128,4096]{2,1,0:T(8,128)(2,1)} %param.7) | copy-start | bytes 3145732
